TPU v7x, 128 devices: a whole 4x4x4 slice. The times are simulated.
128 devices in a mesh: narrow: 2 (over z_hi), wide: 64 (over z_lo, x, y, core).
Axes of the slice: x: 4, y: 4, z: 4 (z_hi: 2, z_lo: 2; z = z_hi * 2 + z_lo), core: 2. Of those that a mesh axis runs over, the one named last changes fastest.
Arguments:
- inputs: bfloat16 [32768, 768], P('wide', 'narrow'), may hold values from -6 to 6
- block_ids: int32 [32768], replicated, may hold values from 0 to 255, never falling along the last dimension, each value on 1 to 256 neighbouring positions
- expert_ids: int32 [32768, 2], P('wide'), may hold values from 0 to 11, all different within a row; in each aligned block of 512 rows (0 to 511, 512 to 1023, ...) at most 128 rows name the same one
- prev_scores: float32 [32768, 12], P('wide'), may hold values from -6 to 6
- gain_one: bfloat16 [768], P('narrow'), may hold values from 0.5 to 1.5
- w_qkv: bfloat16 [768, 2304], P('narrow', 'wide'), may hold values from -0.21875 to 0.21875
- w_out: bfloat16 [768, 768], P('wide', 'narrow'), may hold values from -6 to 6
- gain_two: bfloat16 [768], P('narrow'), may hold values from 0.5 to 1.5
- w_router: bfloat16 [768, 12], P('narrow'), may hold values from -0.15625 to 0.15625
- w_residual: bfloat16 [12, 12], replicated, may hold values from -0.875 to 0.875
- w_const: bfloat16 [768, 4], P('narrow'), may hold values from -0.21875 to 0.21875
- const_vec: bfloat16 [2, 768], P(None, 'narrow'), may hold values from -6 to 6
- w_gate: bfloat16 [768, 16384], P('narrow', 'wide'), may hold values from -0.21875 to 0.21875
- w_up: bfloat16 [768, 16384], P('narrow', 'wide'), may hold values from -0.21875 to 0.21875
- w_down: bfloat16 [16384, 768], P('wide', 'narrow'), may hold values from -0.25 to 0.25
- cotangent: bfloat16 [32768, 768], P('wide', 'narrow'), may hold values from -6 to 6
Outputs:
- layer_out: bfloat16 [32768, 768], P('wide', 'narrow')
- grad_inputs: float32 [32768, 768], P('wide', 'narrow')
- grad_prev: float32 [32768, 12], P('wide')
- grad_gain_one: float32 [768], P('narrow')
- grad_w_qkv: float32 [768, 2304], P('narrow', 'wide')
- grad_w_out: float32 [768, 768], P('wide', 'narrow')
- grad_gain_two: float32 [768], P('narrow')
- grad_w_router: float32 [768, 12], P('narrow')
- grad_w_residual: float32 [12, 12], replicated
- grad_w_const: float32 [768, 4], P('narrow')
- grad_const_vec: float32 [2, 768], P(None, 'narrow')
- grad_w_gate: float32 [768, 16384], P('narrow', 'wide')
- grad_w_up: float32 [768, 16384], P('narrow', 'wide')
- grad_w_down: float32 [16384, 768], P('wide', 'narrow')
Inputs may be any that keep to these rules, and one draw needn't show every extreme that they name: `expert_ids`: each row names two different experts: 0 to 7 are feed-forward experts, 8 the zero expert, 9 the copy expert, 10 and 11 the constant experts. In each aligned block of 512 rows no expert is named by more than 128 rows, a bound that some block reaches. `block_ids`: never falling along the tokens; each id covers 1 to 256 consecutive tokens, one exactly 256.
All inputs are finite; a program needn't handle non-finite values.
Results may differ from a plain program's by a relative error of at most 0.035.
Values may be sent and summed in bfloat16 or wider, within the bound.
A program may use at most 192 MiB of HBM per device.

v0:
```python
import math

import jax
import jax.numpy as jnp
from jax import lax
from jax.sharding import PartitionSpec as P

HEAD_DIM = 64
EXPERTS = 8
SPAN = 8
CAP = 128


epsilon = 1e-06
highest = lax.Precision.HIGHEST
far_block = 1 << 30
masked_score = -1e30


def from_behind(value, axis, steps):
    count = lax.axis_size(axis)
    initial, last = (max(0, -steps), min(count, count - steps))
    return lax.ppermute(value, axis, [(source, source + steps) for source in range(initial, last)])


def exact_dot(left_side, right_side):
    return jnp.dot(left_side, right_side, precision=highest, preferred_element_type=jnp.float32)


def plain_dot(left_side, right_side):
    return jnp.dot(left_side, right_side, preferred_element_type=jnp.float32)


def pair_softmax(logit_pairs):
    pair_top = jnp.max(logit_pairs, axis=-1, keepdims=True)
    pair_exp = jnp.exp(logit_pairs - pair_top)
    return pair_exp / jnp.sum(pair_exp, axis=-1, keepdims=True)


def shards(
    inputs,
    block_ids,
    expert_ids,
    prev_scores,
    gain_one,
    w_qkv,
    w_out,
    gain_two,
    w_router,
    w_residual,
    w_const,
    const_vec,
    w_gate,
    w_up,
    w_down,
    cotangent,
):
    wide_count = lax.axis_size("wide")
    narrow_count = lax.axis_size("narrow")
    wide_index = lax.axis_index("wide")
    narrow_index = lax.axis_index("narrow")
    row_count = inputs.shape[0]
    half_width = inputs.shape[1]
    model_width = half_width * narrow_count
    head_count = half_width // HEAD_DIM
    score_scale = 1.0 / math.sqrt(HEAD_DIM)
    route_count = EXPERTS + 4
    repeat = wide_count // EXPERTS
    qkv_weight, out_weight = (
        lax.all_gather(w_qkv, "wide", axis=1, tiled=True),
        lax.all_gather(w_out, "wide", axis=0, tiled=True),
    )
    inputs_f = inputs.astype(jnp.float32)
    gain_one_f = gain_one.astype(jnp.float32)
    scaled_one = (inputs_f * gain_one_f).astype(jnp.bfloat16)
    project = plain_dot(scaled_one, qkv_weight).reshape(row_count, 3, narrow_count, half_width)
    squares = jnp.sum(inputs_f * inputs_f, axis=1)
    squares_wide = jnp.broadcast_to(squares[:, None], (row_count, narrow_count))
    mine_proj, total_sq = (
        lax.psum_scatter(
            project.astype(jnp.bfloat16), "narrow", scatter_dimension=2, tiled=True
        ).astype(jnp.float32),
        lax.psum_scatter(
            squares_wide.astype(jnp.bfloat16), "narrow", scatter_dimension=1, tiled=True
        ).astype(jnp.float32),
    )
    mine_proj = mine_proj.reshape(row_count, 3, half_width)
    inv_one = lax.rsqrt(total_sq[:, 0] / model_width + epsilon)
    qkv_mine = (inv_one[:, None, None] * mine_proj).astype(jnp.bfloat16)
    queries = qkv_mine[:, 0]
    keys_mine = qkv_mine[:, 1]
    values_mine = qkv_mine[:, 2]
    query_blocks = lax.dynamic_slice_in_dim(block_ids, wide_index * row_count, row_count)
    group_index = wide_index // SPAN
    offsets = [0, -1] + list(range(1, SPAN))
    key_parts = []
    value_parts = []
    block_parts = []
    for offset in offsets:
        if offset == 0:
            shard_keys, shard_values = (keys_mine, values_mine)
        else:
            shard_keys, shard_values = from_behind((keys_mine, values_mine), "wide", offset)
        source = wide_index - offset
        usable = (source >= 0) & (source < wide_count) & (source // SPAN == group_index)
        first_row = jnp.clip(source, 0, wide_count - 1) * row_count
        shard_blocks = lax.dynamic_slice_in_dim(block_ids, first_row, row_count)
        key_parts.append(shard_keys)
        value_parts.append(shard_values)
        block_parts.append(jnp.where(usable, shard_blocks, far_block))
    key_count = len(offsets) * row_count
    keys_heads = (
        jnp.concatenate(key_parts, axis=0)
        .reshape(key_count, head_count, HEAD_DIM)
        .transpose(1, 0, 2)
    )
    values_heads = (
        jnp.concatenate(value_parts, axis=0)
        .reshape(key_count, head_count, HEAD_DIM)
        .transpose(1, 0, 2)
    )
    queries_heads = queries.reshape(row_count, head_count, HEAD_DIM).transpose(1, 0, 2)
    allowed = jnp.concatenate(block_parts)[None, :] <= query_blocks[:, None]

    def head_forward(operands):
        head_queries, head_keys, head_values = operands
        scores = plain_dot(head_queries, head_keys.T) * score_scale
        scores = jnp.where(allowed, scores, masked_score)
        row_top = jnp.max(scores, axis=1, keepdims=True)
        shifted = jnp.exp(scores - row_top)
        row_total = jnp.sum(shifted, axis=1, keepdims=True)
        prob_rows = (shifted / row_total).astype(jnp.bfloat16)
        return (plain_dot(prob_rows, head_values), (row_top + jnp.log(row_total))[:, 0])

    head_outputs, log_totals = lax.map(head_forward, (queries_heads, keys_heads, values_heads))
    attn_mine = head_outputs.transpose(1, 0, 2).reshape(row_count, half_width).astype(jnp.bfloat16)
    attn_full, inputs_full, out_full, gain_two_full, router_full, const_full = (
        lax.all_gather(attn_mine, "narrow", axis=1, tiled=True),
        lax.all_gather(inputs, "narrow", axis=1, tiled=True),
        lax.all_gather(out_weight, "narrow", axis=1, tiled=True),
        lax.all_gather(gain_two, "narrow", axis=0, tiled=True),
        lax.all_gather(w_router, "narrow", axis=0, tiled=True),
        lax.all_gather(w_const, "narrow", axis=0, tiled=True),
    )
    attn_out = plain_dot(attn_full, out_full)
    hidden = inputs_full.astype(jnp.float32) + attn_out
    inv_two = lax.rsqrt(jnp.mean(hidden * hidden, axis=1) + epsilon)
    gain_two_f = gain_two_full.astype(jnp.float32)
    weighted = hidden * gain_two_f
    router_raw = exact_dot(weighted, router_full.astype(jnp.float32))
    const_raw = exact_dot(weighted, const_full.astype(jnp.float32))
    logits = inv_two[:, None] * router_raw + exact_dot(prev_scores, w_residual.astype(jnp.float32))
    const_logit = inv_two[:, None] * const_raw
    normed_full = (hidden * inv_two[:, None] * gain_two_f).astype(jnp.bfloat16)
    column_start = narrow_index * half_width
    normed_half = lax.dynamic_slice_in_dim(normed_full, column_start, half_width, 1)
    hidden_half = lax.dynamic_slice_in_dim(hidden, column_start, half_width, 1)
    gain_two_half = gain_two.astype(jnp.float32)
    route_hot = (expert_ids[:, :, None] == jnp.arange(route_count)[None, None, :]).astype(
        jnp.float32
    )
    chosen = jnp.sum(route_hot * logits[:, None, :], axis=2)
    gate_probs = pair_softmax(chosen)
    const_alpha = pair_softmax(const_logit.reshape(row_count, 2, 2))
    copy_weight = jnp.sum(gate_probs * (expert_ids == EXPERTS + 1), axis=1)
    const_pick = (expert_ids[:, :, None] == EXPERTS + 2 + jnp.arange(2)[None, None, :]).astype(
        jnp.float32
    )
    const_weight = jnp.sum(gate_probs[:, :, None] * const_pick, axis=1)
    self_weight = copy_weight + jnp.sum(const_weight * const_alpha[:, :, 0], axis=1)
    vec_weight = const_weight * const_alpha[:, :, 1]
    pair_ids = expert_ids.reshape(-1)
    pair_hot = (pair_ids[:, None] == jnp.arange(EXPERTS)[None, :]).astype(jnp.int32)
    pair_rank = jnp.sum((jnp.cumsum(pair_hot, axis=0) - 1) * pair_hot, axis=1)
    pair_slot = jnp.where(pair_ids < EXPERTS, pair_ids * CAP + pair_rank, -1).reshape(row_count, 2)
    slot_index = jnp.arange(EXPERTS * CAP)[:, None]
    route_first = (pair_slot[:, 0][None, :] == slot_index).astype(jnp.float32)
    route_second = (pair_slot[:, 1][None, :] == slot_index).astype(jnp.float32)
    route_both = route_first + route_second
    route_gated = route_first * gate_probs[:, 0][None, :] + route_second * gate_probs[:, 1][None, :]
    cotangent_f = cotangent.astype(jnp.float32)
    send_rows = plain_dot(route_both.astype(jnp.bfloat16), normed_half).astype(jnp.bfloat16)
    send_grads = exact_dot(route_gated, cotangent_f).astype(jnp.bfloat16)
    send_rows = jnp.repeat(send_rows.reshape(EXPERTS, CAP, half_width), repeat, axis=0)
    send_grads = jnp.repeat(send_grads.reshape(EXPERTS, CAP, half_width), repeat, axis=0)
    recv_rows, recv_grads = (
        lax.all_to_all(send_rows, "wide", split_axis=0, concat_axis=0, tiled=True),
        lax.all_to_all(send_grads, "wide", split_axis=0, concat_axis=0, tiled=True),
    )
    rows_x = recv_rows.reshape(-1, half_width)
    rows_dy = recv_grads.reshape(-1, half_width)
    gate_block, up_block, down_block = (w_gate, w_up, w_down)
    gate_pre, up_pre, units_grad = (
        lax.psum(plain_dot(rows_x, gate_block).astype(jnp.bfloat16), "narrow").astype(jnp.float32),
        lax.psum(plain_dot(rows_x, up_block).astype(jnp.bfloat16), "narrow").astype(jnp.float32),
        lax.psum(plain_dot(rows_dy, down_block.T).astype(jnp.bfloat16), "narrow").astype(
            jnp.float32
        ),
    )
    sigmoid_gate = jax.nn.sigmoid(gate_pre)
    active = gate_pre * sigmoid_gate
    units_b = (active * up_pre).astype(jnp.bfloat16)
    silu_slope = sigmoid_gate * (1.0 + gate_pre * (1.0 - sigmoid_gate))
    gate_grad = (units_grad * up_pre * silu_slope).astype(jnp.bfloat16)
    up_grad = (units_grad * active).astype(jnp.bfloat16)
    down_part = plain_dot(units_b, down_block)
    back_part = plain_dot(gate_grad, gate_block.T) + plain_dot(up_grad, up_block.T)
    grad_w_gate = plain_dot(rows_x.T, gate_grad)
    grad_w_up = plain_dot(rows_x.T, up_grad)
    grad_w_down = plain_dot(units_b.T, rows_dy)
    back_out, back_grad = (
        lax.all_to_all(
            down_part.reshape(wide_count, -1, half_width).astype(jnp.bfloat16),
            "wide",
            split_axis=0,
            concat_axis=0,
            tiled=True,
        ).astype(jnp.float32),
        lax.all_to_all(
            back_part.reshape(wide_count, -1, half_width).astype(jnp.bfloat16),
            "wide",
            split_axis=0,
            concat_axis=0,
            tiled=True,
        ).astype(jnp.float32),
    )
    ffn_slots = jnp.sum(back_out.reshape(EXPERTS, repeat, CAP, half_width), axis=1).reshape(
        EXPERTS * CAP, half_width
    )
    ffn_slot_grads = jnp.sum(back_grad.reshape(EXPERTS, repeat, CAP, half_width), axis=1).reshape(
        EXPERTS * CAP, half_width
    )
    ffn_first = exact_dot(route_first.T, ffn_slots)
    ffn_second = exact_dot(route_second.T, ffn_slots)
    normed_half_f = normed_half.astype(jnp.float32)
    const_vec_f = const_vec.astype(jnp.float32)
    mixture = (
        gate_probs[:, 0:1] * ffn_first
        + gate_probs[:, 1:2] * ffn_second
        + self_weight[:, None] * normed_half_f
        + exact_dot(vec_weight, const_vec_f)
    )
    layer_out = (hidden_half + mixture).astype(jnp.bfloat16)
    dot_ffn = jnp.stack(
        [jnp.sum(cotangent_f * ffn_first, axis=1), jnp.sum(cotangent_f * ffn_second, axis=1)],
        axis=1,
    )
    dot_self = jnp.sum(cotangent_f * normed_half_f, axis=1)
    dot_vec = exact_dot(cotangent_f, const_vec_f.T)
    normed_grad = exact_dot(route_both.T, ffn_slot_grads) + self_weight[:, None] * cotangent_f
    norm_part = jnp.sum(normed_grad * hidden_half * gain_two_half, axis=1)
    dot_ffn, dot_self, dot_vec, norm_term = lax.psum(
        (dot_ffn, dot_self, dot_vec, norm_part), "narrow"
    )
    const_dot = const_alpha[:, :, 0] * dot_self[:, None] + const_alpha[:, :, 1] * dot_vec
    gate_dots = (
        jnp.where(expert_ids < EXPERTS, dot_ffn, 0.0)
        + (expert_ids == EXPERTS + 1) * dot_self[:, None]
        + jnp.sum(const_pick * const_dot[:, None, :], axis=2)
    )
    chosen_grad = gate_probs * (gate_dots - jnp.sum(gate_probs * gate_dots, axis=1, keepdims=True))
    logits_grad = jnp.sum(chosen_grad[:, :, None] * route_hot, axis=1)
    alpha_grad = const_weight[:, :, None] * jnp.stack(
        [jnp.broadcast_to(dot_self[:, None], dot_vec.shape), dot_vec], axis=2
    )
    const_grad = (
        const_alpha * (alpha_grad - jnp.sum(const_alpha * alpha_grad, axis=2, keepdims=True))
    ).reshape(row_count, 4)
    router_scaled = inv_two[:, None] * logits_grad
    const_scaled = inv_two[:, None] * const_grad
    inv_grad = (
        norm_term
        + jnp.sum(logits_grad * router_raw, axis=1)
        + jnp.sum(const_grad * const_raw, axis=1)
    )
    weighted_grad = exact_dot(router_scaled, w_router.astype(jnp.float32).T) + exact_dot(
        const_scaled, w_const.astype(jnp.float32).T
    )
    weighted_half = hidden_half * gain_two_half
    grad_w_router = exact_dot(weighted_half.T, router_scaled)
    grad_w_const = exact_dot(weighted_half.T, const_scaled)
    grad_w_residual = exact_dot(prev_scores.T, logits_grad)
    grad_prev = exact_dot(logits_grad, w_residual.astype(jnp.float32).T)
    grad_const_vec = exact_dot(vec_weight.T, cotangent_f)
    grad_gain_two = jnp.sum(
        normed_grad * hidden_half * inv_two[:, None] + weighted_grad * hidden_half, axis=0
    )
    inv_two_cube = inv_two * inv_two * inv_two
    hidden_grad = (
        cotangent_f
        + normed_grad * inv_two[:, None] * gain_two_half
        + weighted_grad * gain_two_half
        - (inv_grad * inv_two_cube / model_width)[:, None] * hidden_half
    )
    out_grad_b = hidden_grad.astype(jnp.bfloat16)
    heads_part = plain_dot(out_grad_b, out_weight.T).reshape(row_count, narrow_count, half_width)
    heads_grad = lax.psum_scatter(
        heads_part.astype(jnp.bfloat16), "narrow", scatter_dimension=1, tiled=True
    ).astype(jnp.float32)
    attn_grad = heads_grad.reshape(row_count, half_width).astype(jnp.bfloat16)
    grad_out_part = plain_dot(attn_full.T, out_grad_b)
    attn_grad_heads = attn_grad.reshape(row_count, head_count, HEAD_DIM).transpose(1, 0, 2)

    def head_backward(operands):
        head_queries, head_keys, head_values, head_log, head_out, head_grad = operands
        scores = plain_dot(head_queries, head_keys.T) * score_scale
        prob_rows = jnp.where(allowed, jnp.exp(scores - head_log[:, None]), 0.0)
        prob_grad = plain_dot(head_grad, head_values.T)
        row_term = jnp.sum(head_grad.astype(jnp.float32) * head_out, axis=1, keepdims=True)
        score_grad = (prob_rows * (prob_grad - row_term)).astype(jnp.bfloat16)
        query_grad = plain_dot(score_grad, head_keys) * score_scale
        key_grad = plain_dot(score_grad.T, head_queries) * score_scale
        value_grad = plain_dot(prob_rows.astype(jnp.bfloat16).T, head_grad)
        return (query_grad, key_grad, value_grad)

    query_grads, key_grads, value_grads = lax.map(
        head_backward,
        (queries_heads, keys_heads, values_heads, log_totals, head_outputs, attn_grad_heads),
    )
    query_total = query_grads.transpose(1, 0, 2).reshape(row_count, half_width)
    keys_grad = key_grads.transpose(1, 0, 2).reshape(key_count, half_width)
    values_grad = value_grads.transpose(1, 0, 2).reshape(key_count, half_width)
    key_total = jnp.zeros((row_count, half_width), jnp.float32)
    value_total = jnp.zeros((row_count, half_width), jnp.float32)
    for position, offset in enumerate(offsets):
        part_keys = keys_grad[position * row_count : (position + 1) * row_count]
        part_values = values_grad[position * row_count : (position + 1) * row_count]
        if offset == 0:
            key_total = part_keys
            value_total = part_values
        else:
            back_keys, back_values = (
                from_behind(part_keys.astype(jnp.bfloat16), "wide", -offset).astype(
                    part_keys.dtype
                ),
                from_behind(part_values.astype(jnp.bfloat16), "wide", -offset).astype(
                    part_values.dtype
                ),
            )
            key_total = key_total + back_keys
            value_total = value_total + back_values
    qkv_grad = jnp.stack([query_total, key_total, value_total], axis=1)
    rounded_grad = (inv_one[:, None, None] * qkv_grad).astype(jnp.bfloat16)
    rounded_grad = lax.optimization_barrier(rounded_grad).astype(jnp.float32)
    inv_part = jnp.sum(qkv_grad * mine_proj, axis=(1, 2))
    proj_full, inv_parts = (
        lax.all_gather(rounded_grad.astype(jnp.bfloat16), "narrow", axis=2, tiled=True).astype(
            rounded_grad.dtype
        ),
        lax.all_gather(inv_part[:, None].astype(jnp.bfloat16), "narrow", axis=1, tiled=True).astype(
            jnp.float32
        ),
    )
    proj_grad = proj_full.astype(jnp.bfloat16).reshape(row_count, 3 * model_width)
    scaled_grad = plain_dot(proj_grad, qkv_weight.T)
    grad_qkv_part = plain_dot(scaled_one.T, proj_grad)
    inv_total = jnp.sum(inv_parts, axis=1)
    inv_one_cube = inv_one * inv_one * inv_one
    grad_gain_one = jnp.sum(scaled_grad * inputs_f, axis=0)
    grad_inputs = (
        hidden_grad
        + scaled_grad * gain_one_f
        - (inv_total * inv_one_cube / model_width)[:, None] * inputs_f
    )
    grad_w_qkv, grad_w_out = (
        lax.psum_scatter(grad_qkv_part, "wide", scatter_dimension=1, tiled=True),
        lax.psum_scatter(grad_out_part, "wide", scatter_dimension=0, tiled=True),
    )
    grad_gain_one, grad_gain_two, grad_w_router, grad_w_const, grad_const_vec, grad_w_residual = (
        lax.psum(
            (
                grad_gain_one,
                grad_gain_two,
                grad_w_router,
                grad_w_const,
                grad_const_vec,
                grad_w_residual,
            ),
            "wide",
        )
    )
    return (
        layer_out,
        grad_inputs,
        grad_prev,
        grad_gain_one,
        grad_w_qkv,
        grad_w_out,
        grad_gain_two,
        grad_w_router,
        grad_w_residual,
        grad_w_const,
        grad_const_vec,
        grad_w_gate,
        grad_w_up,
        grad_w_down,
    )


def solution(mesh):
    return jax.shard_map(
        shards,
        mesh=mesh,
        in_specs=(
            P("wide", "narrow"),
            P(),
            P("wide", None),
            P("wide", None),
            P("narrow"),
            P("narrow", "wide"),
            P("wide", "narrow"),
            P("narrow"),
            P("narrow", None),
            P(),
            P("narrow", None),
            P(None, "narrow"),
            P("narrow", "wide"),
            P("narrow", "wide"),
            P("wide", "narrow"),
            P("wide", "narrow"),
        ),
        out_specs=(
            P("wide", "narrow"),
            P("wide", "narrow"),
            P("wide", None),
            P("narrow"),
            P("narrow", "wide"),
            P("wide", "narrow"),
            P("narrow"),
            P("narrow", None),
            P(),
            P("narrow", None),
            P(None, "narrow"),
            P("narrow", "wide"),
            P("narrow", "wide"),
            P("wide", "narrow"),
        ),
        check_vma=False,
    )
```

profile of v0, /device:TPU:7, one launch (start us, length us, event | category | flops | bytes accessed | tf_op | source)
XLA Modules:
  0.0 2191.1 jit_solution(332002092849330883)
XLA Ops:
  8.7 105.8 %all-gather.12.cloned.1.call-done = bf16[64,36,384]{2,1,0:T(8,128)(2,1)} async-done(((bf16[1,36,384]{2,1,0:T(8,128)(2,1)}), bf16[64,36,384]{2,1,0:T(8,128)(2,1)}) %all-gather.12.cloned.1.call-update) | async-done | bytes 1769488 | tf_op jit(solution)/shard_map/all_gather | solution.py:70
  128.8 74.0 %all-gather.1 = bf16[64,12,384]{2,1,0:T(8,128)(2,1)S(1)} all-gather(bf16[1,12,384]{2,1,0:T(8,128)(2,1)S(1)} %bitcast.374), channel_id=1, replica_groups=mesh['narrow'=2,'wide'=64] {'wide'}, dimensions={0}, use_global_device_ids=true | all-gather | bytes 599040 | tf_op jit(solution)/shard_map/all_gather | solution.py:71
  204.1 12.9 all_gather.30
  254.0 6.3 collective-permute-start.11
  260.4 10.6 collective-permute-start.12
  279.5 10.8 collective-permute-start.15
  301.9 5.7 collective-permute-start.2
  308.7 10.1 collective-permute-start.3
  319.8 10.0 collective-permute-start.4
  343.4 6.7 collective-permute-done.2
  357.1 7.9 copy.288
  371.1 7.9 copy.287
  379.0 79.1 %while.28 = (s32[]{:T(128)}, f32[6,512,64]{1,2,0:T(8,128)S(1)}, f32[6,512]{1,0:T(8,128)}, bf16[6,512,64]{2,1,0:T(8,128)(2,1)S(1)}, bf16[6,4608,64]{2,1,0:T(8,128...) while((s32[]{:T(128)}, f32[6,512,64]{1,2,0:T(8,128)S(1)}, ...), condition=%wide.region_6.7_spmd.clone, body=%wide.region_3.6_spmd.clone.sunk | while | flops 625212928 | bytes 68726920 | solution.py:135
  458.8 9.7 all_gather.32
  475.9 41.1 %all-to-all-start = ((bf16[64,128,384]{2,1,0:T(8,128)(2,1)}), bf16[64,128,384]{2,1,0:T(8,128)(2,1)}, u32[]{:S(2)}, u32[]{:S(2)}) async-start(bf16[64,128,384]{2,1,0:T(8,128)(2,1)} %bitcast.314), calls=%async_computation | async-start | bytes 12582912 | tf_op jit(solution)/shard_map/all_to_all | solution.py:187
  517.0 17.4 all_gather.36
  537.7 66.1 %all-to-all-done = bf16[64,128,384]{2,1,0:T(8,128)(2,1)} async-done(((bf16[64,128,384]{2,1,0:T(8,128)(2,1)}), bf16[64,128,384]{2,1,0:T(8,128)(2,1)}, u32[]{:S(2)}, u32[]{:S(2)}) %all-to-all-start) | async-done | bytes 6291488 | tf_op jit(solution)/shard_map/all_to_all | solution.py:187
  607.6 9.8 all-to-all-start.2
  617.4 8.8 all-reduce.15.cloned.1.call-start
  626.2 7.2 convolution_convert_fusion.2
  633.5 7.2 convolution_convert_fusion.3
  640.6 63.6 %all-to-all-done.2 = bf16[64,128,384]{2,1,0:T(8,128)(2,1)} async-done(((bf16[64,128,384]{2,1,0:T(8,128)(2,1)}), bf16[64,128,384]{2,1,0:T(8,128)(2,1)}, u32[]{:S(2)}, u32[]{:S(2)}) %all-to-all-start.2) | async-done | bytes 6291488 | tf_op jit(solution)/shard_map/all_to_all | solution.py:188
  704.2 7.1 convolution_convert_fusion.1
  711.3 300.2 %all-reduce.15.cloned.1.call-done = (bf16[8192,256]{1,0:T(8,128)(2,1)}, bf16[8192,256]{1,0:T(8,128)(2,1)}, bf16[8192,256]{1,0:T(8,128)(2,1)}) async-done(((bf16[8192,256]{1,0:T(8,128)(2,1)}, bf16[8192,256]{1,0:T(8,128)(2,1)}, bf16[8192,256]{1,0:T(8,128)(2,1)}), (bf16[8192,256]{1,0:T(8,128)(2,1)}, bf16[8192,256]{1,0:T(8,128)(2,1)}, bf16[8192,256]{1,0:T(8,128)(2,1)})) %all-reduce.15.cloned.1.call-update) | async-done | bytes 12582928 | tf_op jit(solution)/shard_map/psum | solution.py:195
  1011.5 10.1 fusion.56
  1026.7 8.8 all-to-all-start.1
  1040.2 5.9 add_convert_fusion
  1046.2 76.1 %all-to-all-done.1 = bf16[64,128,384]{2,1,0:T(8,128)(2,1)} async-done(((bf16[64,128,384]{2,1,0:T(8,128)(2,1)}), bf16[64,128,384]{2,1,0:T(8,128)(2,1)}, u32[]{:S(2)}, u32[]{:S(2)}) %all-to-all-start.1) | async-done | bytes 6291488 | tf_op jit(solution)/shard_map/all_to_all | solution.py:212
  1122.3 9.9 all-to-all-start.3
  1132.3 10.0 all_gather.37
  1152.6 18.3 all-reduce.7
  1172.9 46.2 %all-to-all-done.3 = bf16[64,128,384]{2,1,0:T(8,128)(2,1)} async-done(((bf16[64,128,384]{2,1,0:T(8,128)(2,1)}), bf16[64,128,384]{2,1,0:T(8,128)(2,1)}, u32[]{:S(2)}, u32[]{:S(2)}) %all-to-all-start.3) | async-done | bytes 6291488 | tf_op jit(solution)/shard_map/all_to_all | solution.py:219
  1241.5 23.1 %reduce-scatter.9.cloned.1.call-done = bf16[512,1,384]{0,2,1:T(8,128)(2,1)} async-done(((bf16[512,2,384]{0,2,1:T(8,128)(2,1)}), bf16[512,1,384]{0,2,1:T(8,128)(2,1)}) %reduce-scatter.9.cloned.1.call-update) | async-done | bytes 393232 | tf_op jit(solution)/shard_map/reduce_scatter | solution.py:297
  1265.5 152.6 %while.29 = (s32[]{:T(128)}, f32[6,512,64]{1,2,0:T(8,128)}, f32[6,4608,64]{1,2,0:T(8,128)}, f32[6,4608,64]{1,2,0:T(8,128)}, bf16[6,512,64]{2,1,0:T(8,128)(2,1)},...) while((s32[]{:T(128)}, f32[6,512,64]{1,2,0:T(8,128)}, ...), condition=%wide.region_41.42_spmd.clone, body=%wide.region_39.41_spmd.clone.sunk | while | flops 1529249280 | bytes 78220496 | solution.py:316
  1266.3 7.2 exponential_select_fusion.2
  1275.7 6.0 multiply_convert_fusion.4
  1291.8 7.2 exponential_select_fusion.2
  1301.2 6.0 multiply_convert_fusion.4
  1317.2 7.2 exponential_select_fusion.2
  1326.7 6.0 multiply_convert_fusion.4
  1342.6 7.2 exponential_select_fusion.2
  1352.1 6.0 multiply_convert_fusion.4
  1368.0 7.2 exponential_select_fusion.2
  1377.4 6.0 multiply_convert_fusion.4
  1393.5 7.2 exponential_select_fusion.2
  1402.9 6.0 multiply_convert_fusion.4
  1418.2 7.6 bitcast_convert_fusion
  1498.1 8.4 collective-permute-start.27
  1519.4 6.6 fusion.162
  1539.8 8.9 collective-permute-done.28
  1548.7 14.0 collective-permute-done.29
  1562.6 8.4 collective-permute-done.30
  1571.1 11.0 collective-permute-done.31
  1586.3 7.3 fusion.163
  1593.7 5.9 fusion.161
  1603.2 23.7 %all-gather.10.cloned.1.call-done = bf16[512,3,768]{2,0,1:T(8,128)(2,1)} async-done(((bf16[512,3,384]{2,0,1:T(8,128)(2,1)}), bf16[512,3,768]{2,0,1:T(8,128)(2,1)}) %all-gather.10.cloned.1.call-update) | async-done | bytes 2359312 | tf_op jit(solution)/shard_map/all_gather | solution.py:347
  1636.0 143.7 %fusion.152 = (f32[384,48]{0,1:T(8,128)S(1)}, f32[16,384]{1,0:T(8,128)S(1)}) fusion(f32[384,2304]{0,1:T(8,128)} %fusion.114, f32[768,384]{1,0:T(8,128)} %fusion.117), kind=kCustom, calls=%all-reduce-scatter.2 | all-reduce-scatter fusion | flops 1572866 | bytes 4817408
  1786.7 8.7 collective-permute-start.49
  1795.4 14.3 collective-permute-start.50
  1809.7 7.9 collective-permute-start.51
  1880.4 256.2 %all-reduce.6 = (f32[384]{0:T(512)}, f32[384]{0:T(512)}, f32[384,12]{0,1:T(8,128)}, f32[12,12]{0,1:T(8,128)S(1)}, f32[384,4]{0,1:T(4,128)}, /*index=5*/f32[2,384]{1,0:T(2,128)}) all-reduce(f32[384]{0:T(512)S(1)} %get-tuple-element.417, f32[384]{0:T(512)S(1)} %copy-done.56, ...), channel_id=1, replica_groups=mesh['narrow'=2,'wide'=64] {'wide'}, use_global_device_ids=true, to_apply=%region_45.46 | all-reduce | flops 7824 | bytes 62592 | tf_op jit(solution)/shard_map/psum | solution.py:370
  2139.2 14.9 collective-permute-start.42
  2156.0 10.2 collective-permute-start.44
  2174.6 6.0 collective-permute-done.46
  (587 shorter events, 514.1 us)
Async XLA Ops:
  7.2 107.3 %all-gather.12.cloned.1.call-start = ((), (), s32[]{:S(2)}) async-start(), calls=%async_computation.8 | async-start | bytes 1996800 | tf_op jit(solution)/shard_map/all_gather | solution.py:70
  7.9 229.8 %all-reduce.13.cloned.1.call-start = ((), (), s32[]{:S(2)}) async-start(), calls=%async_computation.9 | async-start | bytes 4718592
  128.8 339.8 %all-gather.8.cloned.1.call-start = ((), (), s32[]{:S(2)}) async-start(), calls=%async_computation.5 | async-start | bytes 1769472 | tf_op jit(solution)/shard_map/all_gather | solution.py:140
  240.0 33.6 %collective-permute-start.8 = (bf16[512,384]{1,0:T(8,128)(2,1)S(1)}, bf16[512,384]{1,0:T(8,128)(2,1)S(1)}, u32[]{:S(2)}, u32[]{:S(2)}) collective-permute-start(bf16[512,384]{1,0:T(8,128)(2,1)S(1)} %get-tuple-element.419), channel_id=1, source_target_pairs={{1,0},{2,1},{3,2},{4,3},{5,4},{6,5},{7,6},{8,7},{9,8},{10,9},{11,1... | collective-permute-start | bytes 1179656 | tf_op jit(solution)/shard_map/ppermute | solution.py:23
  244.8 30.9 %collective-permute-start.9 = (bf16[512,384]{1,0:T(8,128)(2,1)S(1)}, bf16[512,384]{1,0:T(8,128)(2,1)S(1)}, u32[]{:S(2)}, u32[]{:S(2)}) collective-permute-start(bf16[512,384]{1,0:T(8,128)(2,1)S(1)} %get-tuple-element.419), channel_id=1, source_target_pairs={{0,1},{1,2},{2,3},{3,4},{4,5},{5,6},{6,7},{7,8},{8,9},{9,10},{10,1... | collective-permute-start | bytes 1179656 | tf_op jit(solution)/shard_map/ppermute | solution.py:23
  249.5 30.0 %collective-permute-start.10 = (bf16[512,384]{1,0:T(8,128)(2,1)S(1)}, bf16[512,384]{1,0:T(8,128)(2,1)}, u32[]{:S(2)}, u32[]{:S(2)}) collective-permute-start(bf16[512,384]{1,0:T(8,128)(2,1)S(1)} %get-tuple-element.419), channel_id=1, source_target_pairs={{0,2},{1,3},{2,4},{3,5},{4,6},{5,7},{6,8},{7,9},{8,10},{9,11},{10,... | collective-permute-start | bytes 1179656 | tf_op jit(solution)/shard_map/ppermute | solution.py:23
  254.0 37.4 %collective-permute-start.11 = (bf16[512,384]{1,0:T(8,128)(2,1)S(1)}, bf16[512,384]{1,0:T(8,128)(2,1)}, u32[]{:S(2)}, u32[]{:S(2)}) collective-permute-start(bf16[512,384]{1,0:T(8,128)(2,1)S(1)} %get-tuple-element.419), channel_id=1, source_target_pairs={{0,3},{1,4},{2,5},{3,6},{4,7},{5,8},{6,9},{7,10},{8,11},{9,12},{10... | collective-permute-start | bytes 1179656 | tf_op jit(solution)/shard_map/ppermute | solution.py:23
  260.4 35.0 %collective-permute-start.12 = (bf16[512,384]{1,0:T(8,128)(2,1)S(1)}, bf16[512,384]{1,0:T(8,128)(2,1)}, u32[]{:S(2)}, u32[]{:S(2)}) collective-permute-start(bf16[512,384]{1,0:T(8,128)(2,1)S(1)} %get-tuple-element.419), channel_id=1, source_target_pairs={{0,4},{1,5},{2,6},{3,7},{4,8},{5,9},{6,10},{7,11},{8,12},{9,13},{1... | collective-permute-start | bytes 1179656 | tf_op jit(solution)/shard_map/ppermute | solution.py:23
  273.6 28.3 %collective-permute-start.13 = (bf16[512,384]{1,0:T(8,128)(2,1)S(1)}, bf16[512,384]{1,0:T(8,128)(2,1)}, u32[]{:S(2)}, u32[]{:S(2)}) collective-permute-start(bf16[512,384]{1,0:T(8,128)(2,1)S(1)} %get-tuple-element.419), channel_id=1, source_target_pairs={{0,5},{1,6},{2,7},{3,8},{4,9},{5,10},{6,11},{7,12},{8,13},{9,14},{... | collective-permute-start | bytes 1179656 | tf_op jit(solution)/shard_map/ppermute | solution.py:23
  275.7 33.0 %collective-permute-start.14 = (bf16[512,384]{1,0:T(8,128)(2,1)S(1)}, bf16[512,384]{1,0:T(8,128)(2,1)S(1)}, u32[]{:S(2)}, u32[]{:S(2)}) collective-permute-start(bf16[512,384]{1,0:T(8,128)(2,1)S(1)} %get-tuple-element.419), channel_id=1, source_target_pairs={{0,6},{1,7},{2,8},{3,9},{4,10},{5,11},{6,12},{7,13},{8,14},{9,15},... | collective-permute-start | bytes 1179656 | tf_op jit(solution)/shard_map/ppermute | solution.py:23
  279.5 40.3 %collective-permute-start.15 = (bf16[512,384]{1,0:T(8,128)(2,1)S(1)}, bf16[512,384]{1,0:T(8,128)(2,1)}, u32[]{:S(2)}, u32[]{:S(2)}) collective-permute-start(bf16[512,384]{1,0:T(8,128)(2,1)S(1)} %get-tuple-element.419), channel_id=1, source_target_pairs={{0,7},{1,8},{2,9},{3,10},{4,11},{5,12},{6,13},{7,14},{8,15},{9,16}... | collective-permute-start | bytes 1179656 | tf_op jit(solution)/shard_map/ppermute | solution.py:23
  291.5 39.6 %collective-permute-start = (bf16[512,384]{1,0:T(8,128)(2,1)S(1)}, bf16[512,384]{1,0:T(8,128)(2,1)}, u32[]{:S(2)}, u32[]{:S(2)}) collective-permute-start(bf16[512,384]{1,0:T(8,128)(2,1)S(1)} %get-tuple-element.420), channel_id=1, source_target_pairs={{1,0},{2,1},{3,2},{4,3},{5,4},{6,5},{7,6},{8,7},{9,8},{10,9},{11,1... | collective-permute-start | bytes 1179656 | tf_op jit(solution)/shard_map/ppermute | solution.py:23
  295.4 42.7 %collective-permute-start.1 = (bf16[512,384]{1,0:T(8,128)(2,1)S(1)}, bf16[512,384]{1,0:T(8,128)(2,1)S(1)}, u32[]{:S(2)}, u32[]{:S(2)}) collective-permute-start(bf16[512,384]{1,0:T(8,128)(2,1)S(1)} %get-tuple-element.420), channel_id=1, source_target_pairs={{0,1},{1,2},{2,3},{3,4},{4,5},{5,6},{6,7},{7,8},{8,9},{9,10},{10,1... | collective-permute-start | bytes 1179656 | tf_op jit(solution)/shard_map/ppermute | solution.py:23
  301.9 48.2 %collective-permute-start.2 = (bf16[512,384]{1,0:T(8,128)(2,1)S(1)}, bf16[512,384]{1,0:T(8,128)(2,1)}, u32[]{:S(2)}, u32[]{:S(2)}) collective-permute-start(bf16[512,384]{1,0:T(8,128)(2,1)S(1)} %get-tuple-element.420), channel_id=1, source_target_pairs={{0,2},{1,3},{2,4},{3,5},{4,6},{5,7},{6,8},{7,9},{8,10},{9,11},{10,... | collective-permute-start | bytes 1179656 | tf_op jit(solution)/shard_map/ppermute | solution.py:23
  308.7 44.7 %collective-permute-start.3 = (bf16[512,384]{1,0:T(8,128)(2,1)S(1)}, bf16[512,384]{1,0:T(8,128)(2,1)}, u32[]{:S(2)}, u32[]{:S(2)}) collective-permute-start(bf16[512,384]{1,0:T(8,128)(2,1)S(1)} %get-tuple-element.420), channel_id=1, source_target_pairs={{0,3},{1,4},{2,5},{3,6},{4,7},{5,8},{6,9},{7,10},{8,11},{9,12},{10... | collective-permute-start | bytes 1179656 | tf_op jit(solution)/shard_map/ppermute | solution.py:23
  319.8 45.1 %collective-permute-start.4 = (bf16[512,384]{1,0:T(8,128)(2,1)S(1)}, bf16[512,384]{1,0:T(8,128)(2,1)S(1)}, u32[]{:S(2)}, u32[]{:S(2)}) collective-permute-start(bf16[512,384]{1,0:T(8,128)(2,1)S(1)} %get-tuple-element.420), channel_id=1, source_target_pairs={{0,4},{1,5},{2,6},{3,7},{4,8},{5,9},{6,10},{7,11},{8,12},{9,13},{1... | collective-permute-start | bytes 1179656 | tf_op jit(solution)/shard_map/ppermute | solution.py:23
  331.0 34.1 %collective-permute-start.5 = (bf16[512,384]{1,0:T(8,128)(2,1)S(1)}, bf16[512,384]{1,0:T(8,128)(2,1)}, u32[]{:S(2)}, u32[]{:S(2)}) collective-permute-start(bf16[512,384]{1,0:T(8,128)(2,1)S(1)} %get-tuple-element.420), channel_id=1, source_target_pairs={{0,5},{1,6},{2,7},{3,8},{4,9},{5,10},{6,11},{7,12},{8,13},{9,14},{... | collective-permute-start | bytes 1179656 | tf_op jit(solution)/shard_map/ppermute | solution.py:23
  338.1 28.2 %collective-permute-start.6 = (bf16[512,384]{1,0:T(8,128)(2,1)S(1)}, bf16[512,384]{1,0:T(8,128)(2,1)}, u32[]{:S(2)}, u32[]{:S(2)}) collective-permute-start(bf16[512,384]{1,0:T(8,128)(2,1)S(1)} %get-tuple-element.420), channel_id=1, source_target_pairs={{0,6},{1,7},{2,8},{3,9},{4,10},{5,11},{6,12},{7,13},{8,14},{9,15},... | collective-permute-start | bytes 1179656 | tf_op jit(solution)/shard_map/ppermute | solution.py:23
  350.1 20.0 collective-permute-start.7
  475.9 128.0 %all-to-all-start = ((bf16[64,128,384]{2,1,0:T(8,128)(2,1)}), bf16[64,128,384]{2,1,0:T(8,128)(2,1)}, u32[]{:S(2)}, u32[]{:S(2)}) async-start(bf16[64,128,384]{2,1,0:T(8,128)(2,1)} %bitcast.314), calls=%async_computation | async-start | bytes 12582912 | tf_op jit(solution)/shard_map/all_to_all | solution.py:187
  607.6 96.6 %all-to-all-start.2 = ((bf16[64,128,384]{2,1,0:T(8,128)(2,1)}), bf16[64,128,384]{2,1,0:T(8,128)(2,1)}, u32[]{:S(2)}, u32[]{:S(2)}) async-start(bf16[64,128,384]{2,1,0:T(8,128)(2,1)} %bitcast.315), calls=%async_computation.2 | async-start | bytes 12582912 | tf_op jit(solution)/shard_map/all_to_all | solution.py:188
  617.4 394.1 %all-reduce.15.cloned.1.call-start = ((), (), s32[]{:S(2)}) async-start(), calls=%async_computation.10 | async-start | bytes 25165824 | tf_op jit(solution)/shard_map/psum | solution.py:195
  1026.7 95.5 %all-to-all-start.1 = ((bf16[64,128,384]{2,1,0:T(8,128)(2,1)}), bf16[64,128,384]{2,1,0:T(8,128)(2,1)}, u32[]{:S(2)}, u32[]{:S(2)}) async-start(bf16[64,128,384]{2,1,0:T(8,128)(2,1)} %bitcast.311), calls=%async_computation.1 | async-start | bytes 12582912 | tf_op jit(solution)/shard_map/all_to_all | solution.py:212
  1122.3 96.8 %all-to-all-start.3 = ((bf16[64,128,384]{2,1,0:T(8,128)(2,1)}), bf16[64,128,384]{2,1,0:T(8,128)(2,1)}, u32[]{:S(2)}, u32[]{:S(2)}) async-start(bf16[64,128,384]{2,1,0:T(8,128)(2,1)} %bitcast.310), calls=%async_computation.3 | async-start | bytes 12582912 | tf_op jit(solution)/shard_map/all_to_all | solution.py:219
  1132.2 132.4 %reduce-scatter.9.cloned.1.call-start = ((), (), s32[]{:S(2)}) async-start(), calls=%async_computation.6 | async-start | bytes 1179648 | tf_op jit(solution)/shard_map/reduce_scatter | solution.py:297
  1241.2 385.7 %all-gather.10.cloned.1.call-start = ((), (), s32[]{:S(2)}) async-start(), calls=%async_computation.7 | async-start | bytes 3538944 | tf_op jit(solution)/shard_map/all_gather | solution.py:347
  1429.4 27.4 %collective-permute-start.16 = (bf16[512,384]{1,0:T(8,128)(2,1)}, bf16[512,384]{1,0:T(8,128)(2,1)}, u32[]{:S(2)}, u32[]{:S(2)}) collective-permute-start(bf16[512,384]{1,0:T(8,128)(2,1)} %copy.306), channel_id=1, source_target_pairs={{0,1},{1,2},{2,3},{3,4},{4,5},{5,6},{6,7},{7,8},{8,9},{9,10},{10,1... | collective-permute-start | bytes 1179656 | tf_op jit(solution)/shard_map/ppermute | solution.py:23
  1435.1 36.1 %collective-permute-start.17 = (bf16[512,384]{1,0:T(8,128)(2,1)}, bf16[512,384]{1,0:T(8,128)(2,1)}, u32[]{:S(2)}, u32[]{:S(2)}) collective-permute-start(bf16[512,384]{1,0:T(8,128)(2,1)} %copy.308), channel_id=1, source_target_pairs={{1,0},{2,1},{3,2},{4,3},{5,4},{6,5},{7,6},{8,7},{9,8},{10,9},{11,1... | collective-permute-start | bytes 1179656 | tf_op jit(solution)/shard_map/ppermute | solution.py:23
  1438.9 35.3 %collective-permute-start.18 = (bf16[512,384]{1,0:T(8,128)(2,1)}, bf16[512,384]{1,0:T(8,128)(2,1)}, u32[]{:S(2)}, u32[]{:S(2)}) collective-permute-start(bf16[512,384]{1,0:T(8,128)(2,1)} %copy.309), channel_id=1, source_target_pairs={{2,0},{3,1},{4,2},{5,3},{6,4},{7,5},{8,6},{9,7},{10,8},{11,9},{12,... | collective-permute-start | bytes 1179656 | tf_op jit(solution)/shard_map/ppermute | solution.py:23
  1445.1 31.1 %collective-permute-start.19 = (bf16[512,384]{1,0:T(8,128)(2,1)}, bf16[512,384]{1,0:T(8,128)(2,1)}, u32[]{:S(2)}, u32[]{:S(2)}) collective-permute-start(bf16[512,384]{1,0:T(8,128)(2,1)} %copy.310), channel_id=1, source_target_pairs={{3,0},{4,1},{5,2},{6,3},{7,4},{8,5},{9,6},{10,7},{11,8},{12,9},{13... | collective-permute-start | bytes 1179656 | tf_op jit(solution)/shard_map/ppermute | solution.py:23
  1450.7 28.4 %collective-permute-start.20 = (bf16[512,384]{1,0:T(8,128)(2,1)}, bf16[512,384]{1,0:T(8,128)(2,1)}, u32[]{:S(2)}, u32[]{:S(2)}) collective-permute-start(bf16[512,384]{1,0:T(8,128)(2,1)} %copy.311), channel_id=1, source_target_pairs={{4,0},{5,1},{6,2},{7,3},{8,4},{9,5},{10,6},{11,7},{12,8},{13,9},{1... | collective-permute-start | bytes 1179656 | tf_op jit(solution)/shard_map/ppermute | solution.py:23
  1456.9 28.8 %collective-permute-start.21 = (bf16[512,384]{1,0:T(8,128)(2,1)}, bf16[512,384]{1,0:T(8,128)(2,1)}, u32[]{:S(2)}, u32[]{:S(2)}) collective-permute-start(bf16[512,384]{1,0:T(8,128)(2,1)} %copy.312), channel_id=1, source_target_pairs={{5,0},{6,1},{7,2},{8,3},{9,4},{10,5},{11,6},{12,7},{13,8},{14,9},{... | collective-permute-start | bytes 1179656 | tf_op jit(solution)/shard_map/ppermute | solution.py:23
  1471.2 26.8 %collective-permute-start.22 = (bf16[512,384]{1,0:T(8,128)(2,1)}, bf16[512,384]{1,0:T(8,128)(2,1)}, u32[]{:S(2)}, u32[]{:S(2)}) collective-permute-start(bf16[512,384]{1,0:T(8,128)(2,1)} %copy.313), channel_id=1, source_target_pairs={{6,0},{7,1},{8,2},{9,3},{10,4},{11,5},{12,6},{13,7},{14,8},{15,9},... | collective-permute-start | bytes 1179656 | tf_op jit(solution)/shard_map/ppermute | solution.py:23
  1474.2 32.2 %collective-permute-start.23 = (bf16[512,384]{1,0:T(8,128)(2,1)}, bf16[512,384]{1,0:T(8,128)(2,1)}, u32[]{:S(2)}, u32[]{:S(2)}) collective-permute-start(bf16[512,384]{1,0:T(8,128)(2,1)} %copy.314), channel_id=1, source_target_pairs={{7,0},{8,1},{9,2},{10,3},{11,4},{12,5},{13,6},{14,7},{15,8},{16,9}... | collective-permute-start | bytes 1179656 | tf_op jit(solution)/shard_map/ppermute | solution.py:23
  1476.2 32.2 %collective-permute-start.24 = (bf16[512,384]{1,0:T(8,128)(2,1)}, bf16[512,384]{1,0:T(8,128)(2,1)}, u32[]{:S(2)}, u32[]{:S(2)}) collective-permute-start(bf16[512,384]{1,0:T(8,128)(2,1)} %copy.315), channel_id=1, source_target_pairs={{0,1},{1,2},{2,3},{3,4},{4,5},{5,6},{6,7},{7,8},{8,9},{9,10},{10,1... | collective-permute-start | bytes 1179656 | tf_op jit(solution)/shard_map/ppermute | solution.py:23
  1479.0 34.9 %collective-permute-start.25 = (bf16[512,384]{1,0:T(8,128)(2,1)}, bf16[512,384]{1,0:T(8,128)(2,1)}, u32[]{:S(2)}, u32[]{:S(2)}) collective-permute-start(bf16[512,384]{1,0:T(8,128)(2,1)} %copy.317), channel_id=1, source_target_pairs={{1,0},{2,1},{3,2},{4,3},{5,4},{6,5},{7,6},{8,7},{9,8},{10,9},{11,1... | collective-permute-start | bytes 1179656 | tf_op jit(solution)/shard_map/ppermute | solution.py:23
  1485.7 31.6 %collective-permute-start.26 = (bf16[512,384]{1,0:T(8,128)(2,1)}, bf16[512,384]{1,0:T(8,128)(2,1)}, u32[]{:S(2)}, u32[]{:S(2)}) collective-permute-start(bf16[512,384]{1,0:T(8,128)(2,1)} %copy.318), channel_id=1, source_target_pairs={{2,0},{3,1},{4,2},{5,3},{6,4},{7,5},{8,6},{9,7},{10,8},{11,9},{12,... | collective-permute-start | bytes 1179656 | tf_op jit(solution)/shard_map/ppermute | solution.py:23
  1498.1 41.7 %collective-permute-start.27 = (bf16[512,384]{1,0:T(8,128)(2,1)}, bf16[512,384]{1,0:T(8,128)(2,1)S(1)}, u32[]{:S(2)}, u32[]{:S(2)}) collective-permute-start(bf16[512,384]{1,0:T(8,128)(2,1)} %copy.319), channel_id=1, source_target_pairs={{3,0},{4,1},{5,2},{6,3},{7,4},{8,5},{9,6},{10,7},{11,8},{12,9},{13... | collective-permute-start | bytes 1179656 | tf_op jit(solution)/shard_map/ppermute | solution.py:23
  1506.4 42.2 %collective-permute-start.28 = (bf16[512,384]{1,0:T(8,128)(2,1)}, bf16[512,384]{1,0:T(8,128)(2,1)}, u32[]{:S(2)}, u32[]{:S(2)}) collective-permute-start(bf16[512,384]{1,0:T(8,128)(2,1)} %copy.320), channel_id=1, source_target_pairs={{4,0},{5,1},{6,2},{7,3},{8,4},{9,5},{10,6},{11,7},{12,8},{13,9},{1... | collective-permute-start | bytes 1179656 | tf_op jit(solution)/shard_map/ppermute | solution.py:23
  1508.4 54.3 %collective-permute-start.29 = (bf16[512,384]{1,0:T(8,128)(2,1)}, bf16[512,384]{1,0:T(8,128)(2,1)}, u32[]{:S(2)}, u32[]{:S(2)}) collective-permute-start(bf16[512,384]{1,0:T(8,128)(2,1)} %copy.321), channel_id=1, source_target_pairs={{5,0},{6,1},{7,2},{8,3},{9,4},{10,5},{11,6},{12,7},{13,8},{14,9},{... | collective-permute-start | bytes 1179656 | tf_op jit(solution)/shard_map/ppermute | solution.py:23
  1513.9 57.2 %collective-permute-start.30 = (bf16[512,384]{1,0:T(8,128)(2,1)}, bf16[512,384]{1,0:T(8,128)(2,1)}, u32[]{:S(2)}, u32[]{:S(2)}) collective-permute-start(bf16[512,384]{1,0:T(8,128)(2,1)} %copy.322), channel_id=1, source_target_pairs={{6,0},{7,1},{8,2},{9,3},{10,4},{11,5},{12,6},{13,7},{14,8},{15,9},... | collective-permute-start | bytes 1179656 | tf_op jit(solution)/shard_map/ppermute | solution.py:23
  1517.3 64.8 %collective-permute-start.31 = (bf16[512,384]{1,0:T(8,128)(2,1)}, bf16[512,384]{1,0:T(8,128)(2,1)}, u32[]{:S(2)}, u32[]{:S(2)}) collective-permute-start(bf16[512,384]{1,0:T(8,128)(2,1)} %copy.323), channel_id=1, source_target_pairs={{7,0},{8,1},{9,2},{10,3},{11,4},{12,5},{13,6},{14,7},{15,8},{16,9}... | collective-permute-start | bytes 1179656 | tf_op jit(solution)/shard_map/ppermute | solution.py:23
  1779.7 40.0 %collective-permute-start.48 = (f32[16,384]{1,0:T(8,128)S(1)}, f32[16,384]{1,0:T(8,128)S(1)}, u32[]{:S(2)}, u32[]{:S(2)}) collective-permute-start(f32[16,384]{1,0:T(8,128)S(1)} %get-tuple-element.390), channel_id=1, source_target_pairs={{0,1},{1,2},{2,3},{3,4},{4,5},{5,6},{6,7},{7,8},{8,9},{9,10},{10,1... | collective-permute-start | bytes 73736
  1784.0 33.5 %collective-permute-start.63 = (f32[12,384]{1,0:T(8,128)S(1)}, f32[12,384]{1,0:T(8,128)S(1)}, u32[]{:S(2)}, u32[]{:S(2)}) collective-permute-start(f32[12,384]{1,0:T(8,128)S(1)} %slice.189), channel_id=1, source_target_pairs={{0,16},{1,17},{2,18},{3,19},{4,20},{5,21},{6,22},{7,23},{8,24},{9,... | collective-permute-start | bytes 55304
  1786.7 35.5 %collective-permute-start.49 = (f32[16,384]{1,0:T(8,128)S(1)}, f32[16,384]{1,0:T(8,128)S(1)}, u32[]{:S(2)}, u32[]{:S(2)}) collective-permute-start(f32[16,384]{1,0:T(8,128)S(1)} %get-tuple-element.390), channel_id=1, source_target_pairs={{0,2},{1,3},{2,4},{3,5},{4,6},{5,7},{6,8},{7,9},{8,10},{9,11},{10,... | collective-permute-start | bytes 73736
  1795.4 29.1 %collective-permute-start.50 = (f32[16,384]{1,0:T(8,128)S(1)}, f32[16,384]{1,0:T(8,128)S(1)}, u32[]{:S(2)}, u32[]{:S(2)}) collective-permute-start(f32[16,384]{1,0:T(8,128)S(1)} %get-tuple-element.390), channel_id=1, source_target_pairs={{0,3},{1,4},{2,5},{3,6},{4,7},{5,8},{6,9},{7,10},{8,11},{9,12},{10... | collective-permute-start | bytes 73736
  1809.7 16.8 collective-permute-start.51
  1822.2 16.1 collective-permute-start.54
  1824.5 17.2 collective-permute-start.55
  1826.5 18.2 collective-permute-start.56
  1829.2 17.4 collective-permute-start.57
  1831.2 17.4 collective-permute-start.58
  1850.5 15.6 collective-permute-start.32
  1853.3 14.8 collective-permute-start.33
  1855.2 14.8 collective-permute-start.34
  1858.6 13.3 collective-permute-start.35
  1866.1 273.1 %collective-permute-start.37 = (f32[384,48]{0,1:T(8,128)S(1)}, f32[384,48]{0,1:T(8,128)S(1)}, u32[]{:S(2)}, u32[]{:S(2)}) collective-permute-start(f32[384,48]{0,1:T(8,128)S(1)} %get-tuple-element.389), channel_id=1, source_target_pairs={{0,6},{1,7},{2,8},{3,9},{4,10},{5,11},{6,12},{7,13},{8,14},{9,15},... | collective-permute-start | bytes 221192
  1868.0 286.1 %collective-permute-start.38 = (f32[384,48]{0,1:T(8,128)S(1)}, f32[384,48]{0,1:T(8,128)S(1)}, u32[]{:S(2)}, u32[]{:S(2)}) collective-permute-start(f32[384,48]{0,1:T(8,128)S(1)} %get-tuple-element.389), channel_id=1, source_target_pairs={{0,7},{1,8},{2,9},{3,10},{4,11},{5,12},{6,13},{7,14},{8,15},{9,16}... | collective-permute-start | bytes 221192
  1870.0 286.1 %collective-permute-start.39 = (f32[384,48]{0,1:T(8,128)S(1)}, f32[384,48]{0,1:T(8,128)S(1)}, u32[]{:S(2)}, u32[]{:S(2)}) collective-permute-start(f32[384,48]{0,1:T(8,128)S(1)} %get-tuple-element.389), channel_id=1, source_target_pairs={{0,8},{1,9},{2,10},{3,11},{4,12},{5,13},{6,14},{7,15},{8,16},{9,17... | collective-permute-start | bytes 221192
  1871.9 294.4 %collective-permute-start.40 = (f32[384,48]{0,1:T(8,128)S(1)}, f32[384,48]{0,1:T(8,128)S(1)}, u32[]{:S(2)}, u32[]{:S(2)}) collective-permute-start(f32[384,48]{0,1:T(8,128)S(1)} %get-tuple-element.389), channel_id=1, source_target_pairs={{0,9},{1,10},{2,11},{3,12},{4,13},{5,14},{6,15},{7,16},{8,17},{9,1... | collective-permute-start | bytes 221192
  1873.8 297.9 %collective-permute-start.41 = (f32[384,48]{0,1:T(8,128)S(1)}, f32[384,48]{0,1:T(8,128)S(1)}, u32[]{:S(2)}, u32[]{:S(2)}) collective-permute-start(f32[384,48]{0,1:T(8,128)S(1)} %get-tuple-element.389), channel_id=1, source_target_pairs={{0,10},{1,11},{2,12},{3,13},{4,14},{5,15},{6,16},{7,17},{8,18},{9,... | collective-permute-start | bytes 221192
  2139.2 35.4 %collective-permute-start.42 = (f32[384,48]{0,1:T(8,128)S(1)}, f32[384,48]{0,1:T(8,128)S(1)}, u32[]{:S(2)}, u32[]{:S(2)}) collective-permute-start(f32[384,48]{0,1:T(8,128)S(1)} %get-tuple-element.389), channel_id=1, source_target_pairs={{0,11},{1,12},{2,13},{3,14},{4,15},{5,16},{6,17},{7,18},{8,19},{9,... | collective-permute-start | bytes 221192
  2154.1 20.5 collective-permute-start.43
  2156.0 18.6 collective-permute-start.44
  (103 other events, 4693.2 us)
Sparse Core Ops, SparseCore 0:
  9.8 104.6 all-gather.11
  128.9 77.7 all-reduce.12
  208.4 29.5 all-gather.7
  711.5 300.0 all-reduce.14
  1241.3 23.1 reduce-scatter.8
  1586.4 40.4 all-gather.9
where the time goes:
time: 2210 us; the launch traced here: 2190 us
  waiting for transfers between devices  767 us (35%)
  blocking collectives  562 us (25%)
  starting transfers between devices  339 us (15%)
  matrix products  281 us (13%)
  local copies, waits for them, and re-layouts  165 us (7%)
  other arithmetic  57.9 us (3%)
    psum x1, waiting for transfers between devices, shards(): lax.psum(plain_dot(rows_x, up_block).astype(jnp.bfloat16), 'narrow')  300 us
    dot_general x58, matrix products, plain_dot(): return jnp.dot(left_side, right_side, preferred_element_type=jnp.float32)  261 us
    psum x1, blocking collectives, shards(): lax.psum((grad_gain_one, grad_gain_two, grad_w_router, grad_w_const, grad...  256 us
    unnamed x2, blocking collectives  149 us
    ppermute x32, starting transfers between devices, from_behind(): lax.ppermute(value, axis, [(source, source + steps) for source in range(i...  137 us
    unnamed x33, starting transfers between devices  123 us
    all_gather x1, waiting for transfers between devices, shards(): lax.all_gather(w_qkv, 'wide', axis=1, tiled=True)  106 us
    all_to_all x1, waiting for transfers between devices, shards(): lax.all_to_all(down_part.reshape(wide_count, -1, half_width).astype(jnp.b...  76.1 us
  transfers between devices with their start and end apart: 74, of which 16 were waited for; matrix products, arithmetic and copies ran while one was open for 11% of the time, Pallas kernels for 0%

commit v1 on v0

v1 whole, which is shorter than its diff:
```python
import functools
import math

import jax
import jax.numpy as jnp
from jax import lax
from jax.experimental import pallas as pl
from jax.experimental.pallas import tpu as pltpu
from jax.sharding import Mesh
from jax.sharding import PartitionSpec as P

HEAD_DIM = 64
EXPERTS = 8
ROUTES = 12
CAP = 128
D = 768
HALF = 384
TOK = 256
SEQ = 4096
KT = 512

MESH = pl.DeviceIdType.MESH
AXES = ("n", "zl", "x", "y", "c")
SIZES = dict(n=2, zl=2, x=4, y=4, c=2, z=4)
WIDE = ("zl", "x", "y", "c")
VMEM_LIMIT = 60 * 1024 * 1024

epsilon = 1e-06
highest = lax.Precision.HIGHEST
f32 = jnp.float32
bf16 = jnp.bfloat16


def exact_dot(left_side, right_side):
    return jnp.dot(left_side, right_side, precision=highest, preferred_element_type=f32)


def dot_dims(left_side, right_side, left_dim, right_dim):
    return lax.dot_general(
        left_side, right_side, (((left_dim,), (right_dim,)), ((), ())), preferred_element_type=f32
    )


def pair_softmax(logit_pairs):
    pair_top = jnp.max(logit_pairs, axis=-1, keepdims=True)
    pair_exp = jnp.exp(logit_pairs - pair_top)
    return pair_exp / jnp.sum(pair_exp, axis=-1, keepdims=True)


def coords():
    place = {axis: lax.axis_index(axis) for axis in AXES}
    place["z"] = place["n"] * 2 + place["zl"]
    return place


def moved(place, shift):
    target = {}
    for axis, steps in shift.items():
        value = lax.rem(place[axis] + steps, SIZES[axis])
        if axis == "z":
            target["n"] = value // 2
            target["zl"] = lax.rem(value, 2)
        else:
            target[axis] = value
    return target


def shifts_of(axes):
    found = [{}]
    for axis in axes:
        found = [dict(one, **{axis: k}) for one in found for k in range(SIZES[axis])]
    return [{a: k for a, k in one.items() if k} for one in found if any(one.values())]


def reverse(shift):
    return {axis: (SIZES[axis] - steps) % SIZES[axis] for axis, steps in shift.items()}


def rank_of(place, axes, shift=None):
    rank = 0
    for axis in axes:
        value = place[axis]
        if shift and axis in shift:
            value = lax.rem(value + shift[axis], SIZES[axis])
        rank = rank * SIZES[axis] + value
    return rank


def greet_start(place, shifts):
    barrier = pltpu.get_barrier_semaphore()
    for shift in shifts:
        pl.semaphore_signal(barrier, inc=1, device_id=moved(place, shift), device_id_type=MESH)


def greet_end(shifts):
    pl.semaphore_wait(pltpu.get_barrier_semaphore(), len(shifts))


def greet(place, shifts):
    greet_start(place, shifts)
    greet_end(shifts)


def push(source, target, send_sem, recv_sem, device):
    copy = pltpu.make_async_remote_copy(
        src_ref=source,
        dst_ref=target,
        send_sem=send_sem,
        recv_sem=recv_sem,
        device_id=device,
        device_id_type=MESH,
    )
    copy.start()
    return copy


def in_vmem(count):
    return [pl.BlockSpec(memory_space=pltpu.VMEM)] * count


def comm_params(collective_id):
    return pltpu.CompilerParams(
        collective_id=collective_id, has_side_effects=True, vmem_limit_bytes=VMEM_LIMIT
    )


def shape_of(shape, dtype):
    return jax.ShapeDtypeStruct(shape, dtype)


def unique(shift_lists):
    seen = []
    for shifts in shift_lists:
        for shift in shifts:
            if shift not in seen:
                seen.append(shift)
    return seen


def diagonal(size):
    rows = lax.broadcasted_iota(jnp.int32, (size, size), 0)
    return rows == lax.broadcasted_iota(jnp.int32, (size, size), 1)


def to_row(value):
    size = value.shape[0]
    return jnp.sum(jnp.where(diagonal(size), value, jnp.zeros_like(value)), axis=0, keepdims=True)


def to_column(value):
    size = min(value.shape[1], 128)
    mask = diagonal(size)
    return jnp.concatenate(
        [
            jnp.sum(
                jnp.where(mask, value[:, k * size : (k + 1) * size], jnp.zeros((), value.dtype)),
                axis=1,
                keepdims=True,
            )
            for k in range(value.shape[1] // size)
        ],
        axis=0,
    )


ORDERS = (("x", "y", "z"), ("y", "z", "x"), ("z", "x", "y"))
PART = 16


def make_plan(ids_ref, cot_ref, hit_ref, table_ref, rows_ref):
    tokens = 2 * TOK
    expert = lax.broadcasted_iota(jnp.int32, (tokens, 128), 1)
    ids = [to_column(ids_ref[k : k + 1, :]) for k in range(2)]
    table_ref[...] = jnp.zeros_like(table_ref)
    named = ((expert == ids[0]) | (expert == ids[1])).astype(bf16)
    before = lax.broadcasted_iota(jnp.int32, (tokens, tokens), 1) < lax.broadcasted_iota(
        jnp.int32, (tokens, tokens), 0
    )
    ranks = dot_dims(before.astype(bf16), named, 1, 0)
    slot = lax.broadcasted_iota(jnp.int32, (CAP * 2, tokens), 0)
    rows = []
    for k in range(2):
        rank = jnp.sum(jnp.where(expert == ids[k], ranks, 0.0), axis=1, keepdims=True)
        place = jnp.where(ids[k] < EXPERTS, ids[k] * CAP + rank.astype(jnp.int32), -1)
        table_ref[:, k : k + 1] = ids[k]
        table_ref[:, 2 + k : 3 + k] = place
        rows.append(to_row(place))
    for j in range(4):
        first = j * 2 * CAP
        hit = ((slot + first == rows[0]) | (slot + first == rows[1])).astype(bf16)
        hit_ref[first : first + 2 * CAP, :] = hit
        held = dot_dims(hit[:, :TOK], cot_ref[0], 1, 0) + dot_dims(hit[:, TOK:], cot_ref[1], 1, 0)
        held = held.astype(bf16)
        for i in range(4):
            rows_ref[j * 4 + i] = held[i * 64 : (i + 1) * 64, :]


def gather_all(w_qkv, w_out, inputs, cotangent, gains, tables, expert_ids):
    swaps_in = [
        (inputs, 1),
        (cotangent, 1),
        (shape_of((1, PART, HALF), bf16), 2),
        (shape_of((1, HALF, 128), bf16), 2),
    ]
    extra = len(swaps_in)
    given = [w_qkv, w_out, inputs, cotangent, expert_ids, *gains, *tables]
    peers = unique([shifts_of((a,)) for a in ("x", "y", "z", "c")])

    def kernel(*refs):
        qkv_ref, out_ref, in_ref, cot_ref, ids_ref = refs[:5]
        small_refs = refs[5 : len(given)]
        rest = refs[len(given) :]
        parts, swapped = rest[:3], rest[3 : 3 + extra]
        hit_ref, slots_ref, rows_ref = rest[3 + extra : 6 + extra]
        gain_s, table_s, send, recv, sib_send, sib_recv, swap_send, swap_recv = rest[6 + extra :]
        ins = (in_ref, cot_ref, gain_s, table_s)
        place = coords()
        core = place["c"]
        block = jnp.concatenate([qkv_ref[...].astype(f32), out_ref[...].astype(f32)], axis=0)
        block = block.astype(bf16)
        for k in range(3):
            first, second, third = (place[a] for a in ORDERS[k])
            parts[k][core, third, second, first] = block[k * PART : (k + 1) * PART, :]
        greet_start(place, peers)
        rows = [ref[...].astype(f32) for ref in small_refs[: len(gains)]]
        rows.append(jnp.zeros((PART - sum(row.shape[0] for row in rows), HALF), f32))
        gain_s[0] = jnp.concatenate(rows, axis=0).astype(bf16)
        lanes = [ref[...].astype(f32) for ref in small_refs[len(gains) :]]
        lanes.append(jnp.zeros((128 - sum(lane.shape[0] for lane in lanes), HALF), f32))
        table_s[0] = jnp.concatenate(lanes, axis=0).T.astype(bf16)
        greet_end(peers)
        stages = []
        for k in range(3):
            first, second, third = (place[a] for a in ORDERS[k])
            spot = parts[k].at[core, third, second, first]
            stages.append(
                [
                    push(spot, spot, send.at[k, 0, d], recv.at[k, 0, d], moved(place, {ORDERS[k][0]: d + 1}))
                    for d in range(3)
                ]
            )
        swaps = swap_start(place, swaps_in, ins, swapped, swap_send, swap_recv)
        make_plan(ids_ref, cot_ref, hit_ref, slots_ref, rows_ref)
        later = []
        for k in range(3):
            first, second, third = (place[a] for a in ORDERS[k])
            for copy in stages[k]:
                copy.wait_recv()
            spot = parts[k].at[core, third, second]
            later.append(
                [
                    push(spot, spot, send.at[k, 1, d], recv.at[k, 1, d], moved(place, {ORDERS[k][1]: d + 1}))
                    for d in range(3)
                ]
            )
        last, sibling = [], []
        for k in range(3):
            third = place[ORDERS[k][2]]
            for copy in later[k]:
                copy.wait_recv()
            spot = parts[k].at[core, third]
            last.append(
                [
                    push(spot, spot, send.at[k, 2, d], recv.at[k, 2, d], moved(place, {ORDERS[k][2]: d + 1}))
                    for d in range(3)
                ]
            )
            sibling.append(push(spot, spot, sib_send.at[k, 0], sib_recv.at[k, 0], moved(place, {"c": 1})))
        for d in range(3):
            for k in range(3):
                third = place[ORDERS[k][2]]
                last[k][d].wait_recv()
                spot = parts[k].at[core, lax.rem(third + 3 - d, 4)]
                sibling.append(
                    push(spot, spot, sib_send.at[k, d + 1], sib_recv.at[k, d + 1], moved(place, {"c": 1}))
                )
        for copy in sibling + swaps:
            copy.wait_recv()
        for k in range(3):
            for copy in stages[k] + later[k] + last[k]:
                copy.wait_send()
        for copy in sibling + swaps:
            copy.wait_send()

    whole = shape_of((2, 4, 4, 4, PART, HALF), bf16)
    return pl.pallas_call(
        kernel,
        out_shape=[whole] * 3
        + swap_shapes(swaps_in)
        + [
            shape_of((EXPERTS * CAP, 2 * TOK), bf16),
            shape_of((2 * TOK, 128), jnp.int32),
            shape_of((16, 64, HALF), bf16),
        ],
        in_specs=in_vmem(len(given)),
        out_specs=in_vmem(6 + extra),
        scratch_shapes=[
            pltpu.VMEM((1, PART, HALF), bf16),
            pltpu.VMEM((1, HALF, 128), bf16),
            pltpu.SemaphoreType.DMA((3, 3, 3)),
            pltpu.SemaphoreType.DMA((3, 3, 3)),
            pltpu.SemaphoreType.DMA((3, 4)),
            pltpu.SemaphoreType.DMA((3, 4)),
            pltpu.SemaphoreType.DMA((extra,)),
            pltpu.SemaphoreType.DMA((extra,)),
        ],
        compiler_params=comm_params(1),
        name="gather_weights",
    )(*given)


def swap_shapes(swaps_in):
    return [shape_of((2,) + a.shape[1:], a.dtype) for a, _ in swaps_in]


def swap_start(place, swaps_in, ins, swapped, send, recv):
    n = place["n"]
    copies = []
    for i, (_, share) in enumerate(swaps_in):
        copies.append(
            push(ins[i].at[(1 - n) // share], swapped[i].at[n], send.at[i], recv.at[i], moved(place, {"z": 2}))
        )
        swapped[i][n] = ins[i][n // share]
    return copies


def blocks_of_weights():
    for zl in range(2):
        for x in range(4):
            for y in range(4):
                for c in range(2):
                    for n in range(2):
                        at = dict(x=x, y=y, z=2 * n + zl)
                        spots = [(c, at[o[2]], at[o[1]], at[o[0]]) for o in ORDERS]
                        yield ((zl * 4 + x) * 4 + y) * 2 + c, slice(n * HALF, (n + 1) * HALF), spots


def project_forward(parts, x_halves, vectors):
    def kernel(pa, pb, pc, x_ref, vec_ref, wq_ref, wo_ref, q_ref, kv_ref, pq_ref, proj_ref, scaled_ref, inv_ref, wq_s, wo_s):
        parts = (pa, pb, pc)
        for w, cols, spots in blocks_of_weights():
            blocks = [parts[k][spots[k]].astype(f32) for k in range(3)]
            wq_s[w * 36 : w * 36 + 16, cols] = blocks[0]
            wq_s[w * 36 + 16 : w * 36 + 32, cols] = blocks[1]
            wq_s[w * 36 + 32 : w * 36 + 36, cols] = blocks[2][:4]
            wo_s[w * 12 : w * 12 + 12, cols] = blocks[2][4:]
        for j in range(9):
            wq_ref[j * 256 : (j + 1) * 256, :] = wq_s[j * 256 : (j + 1) * 256, :].astype(bf16)
        for j in range(3):
            wo_ref[j * 256 : (j + 1) * 256, :] = wo_s[j * 256 : (j + 1) * 256, :].astype(bf16)
        x = jnp.concatenate([x_ref[0], x_ref[1]], axis=1).astype(f32)
        gain = jnp.concatenate([vec_ref[0, 0:1], vec_ref[1, 0:1]], axis=1).astype(f32)
        inv = lax.rsqrt(jnp.mean(x * x, axis=1, keepdims=True) + epsilon)
        scaled = (x * gain).astype(bf16)
        scaled_ref[...] = scaled
        inv_ref[...] = inv
        inv_row = to_row(inv)
        for s in range(3):
            for y in range(4):
                first = s * D + y * 192
                if s == 0:
                    project = dot_dims(wq_ref[first : first + 192, :], scaled, 1, 1)
                    pq_ref[y] = project
                    q_ref[y] = (inv_row * project).astype(bf16)
                else:
                    project = dot_dims(scaled, wq_ref[first : first + 192, :], 1, 1)
                    proj_ref[(s - 1) * 4 + y] = project
                    value = (inv * project).astype(bf16)
                    for h in range(3):
                        spot = h * 128 + (s - 1) * HEAD_DIM
                        kv_ref[y, :, spot : spot + HEAD_DIM] = value[:, h * HEAD_DIM : (h + 1) * HEAD_DIM]

    return pl.pallas_call(
        kernel,
        out_shape=[
            shape_of((3 * D, D), bf16),
            shape_of((D, D), bf16),
            shape_of((4, 192, TOK), bf16),
            shape_of((4, TOK, HALF), bf16),
            shape_of((4, 192, TOK), f32),
            shape_of((8, TOK, 192), f32),
            shape_of((TOK, D), bf16),
            shape_of((TOK, 1), f32),
        ],
        in_specs=in_vmem(5),
        out_specs=in_vmem(8),
        scratch_shapes=[pltpu.VMEM((3 * D, D), f32), pltpu.VMEM((D, D), f32)],
        compiler_params=pltpu.CompilerParams(vmem_limit_bytes=VMEM_LIMIT),
        name="project_forward",
    )(*parts, x_halves, vectors)


SCALARS = ("inv", "gate0", "gate1", "a00", "a01", "a10", "a11", "cw0", "cw1", "self", "vec0", "vec1")
RAW = 32


def column(table, name):
    spot = SCALARS.index(name)
    return table[:, spot : spot + 1]


def vector_rows(vec_ref, first, count):
    both = [vec_ref[half, first : first + count].astype(f32) for half in range(2)]
    return jnp.concatenate(both, axis=1)


def exact_dims(left_side, right_side, left_dim, right_dim):
    return lax.dot_general(
        left_side,
        right_side,
        (((left_dim,), (right_dim,)), ((), ())),
        precision=highest,
        preferred_element_type=f32,
    )


def router_table(rc_ref):
    return jnp.concatenate([rc_ref[half, :, :16].astype(f32) for half in range(2)], axis=0)


def middle_forward(
    own_tokens, at_ref, x_ref, wo_ref, vec_ref, rc_ref, prev_ref, res_ref, plan_ref,
    hidden_ref, normed_ref, base_ref, table_ref, gates_ref,
):
    hidden = jnp.concatenate([x_ref[0], x_ref[1]], axis=1).astype(f32)
    for y in range(4):
        hidden = hidden + dot_dims(at_ref[y], wo_ref[y * 192 : (y + 1) * 192, :], 0, 0)
    hidden_ref[...] = hidden
    gain = vector_rows(vec_ref, 1, 1)
    inv = lax.rsqrt(jnp.mean(hidden * hidden, axis=1, keepdims=True) + epsilon)
    weighted = hidden * gain
    normed = (hidden * inv * gain).astype(bf16)
    normed_ref[...] = normed
    raw = exact_dims(weighted, router_table(rc_ref), 1, 0)
    logits = inv * raw[:, :ROUTES] + exact_dims(prev_ref[:, own_tokens], res_ref[...].astype(f32), 0, 0)
    route = lax.broadcasted_iota(jnp.int32, (TOK, ROUTES), 1)
    e0, e1 = plan_ref[own_tokens, 0:1], plan_ref[own_tokens, 1:2]
    l0 = jnp.sum(jnp.where(route == e0, logits, 0.0), axis=1, keepdims=True)
    l1 = jnp.sum(jnp.where(route == e1, logits, 0.0), axis=1, keepdims=True)

    def softmax_two(first, second):
        top = jnp.maximum(first, second)
        a, b = jnp.exp(first - top), jnp.exp(second - top)
        return a / (a + b), b / (a + b)

    gate0, gate1 = softmax_two(l0, l1)
    coeff = [inv * raw[:, ROUTES + i : ROUTES + i + 1] for i in range(4)]
    a00, a01 = softmax_two(coeff[0], coeff[1])
    a10, a11 = softmax_two(coeff[2], coeff[3])

    def chosen(expert):
        return jnp.where(e0 == expert, gate0, 0.0) + jnp.where(e1 == expert, gate1, 0.0)

    cw0, cw1 = chosen(EXPERTS + 2), chosen(EXPERTS + 3)
    own = chosen(EXPERTS + 1) + cw0 * a00 + cw1 * a10
    vec0, vec1 = cw0 * a01, cw1 * a11
    const = vector_rows(vec_ref, 2, 2)
    base = hidden + own * normed.astype(f32) + vec0 * const[0:1] + vec1 * const[1:2]
    for half in range(2):
        base_ref[half] = base[:, half * HALF : (half + 1) * HALF].astype(bf16)
    values = dict(
        inv=inv, gate0=gate0, gate1=gate1, a00=a00, a01=a01, a10=a10, a11=a11, cw0=cw0, cw1=cw1,
        self=own, vec0=vec0, vec1=vec1,
    )
    lane = lax.broadcasted_iota(jnp.int32, (TOK, 128), 1)
    table = jnp.zeros((TOK, 128), f32)
    for i, name in enumerate(SCALARS):
        table = jnp.where(lane == i, values[name], table)
    table_ref[...] = table
    table_ref[:, RAW : RAW + 16] = raw
    slot = lax.broadcasted_iota(jnp.int32, (TOK, EXPERTS * CAP), 1)
    s0, s1 = plan_ref[own_tokens, 2:3], plan_ref[own_tokens, 3:4]
    slot_gates = jnp.where(slot == s0, gate0, 0.0) + jnp.where(slot == s1, gate1, 0.0)
    slot_gates = jnp.sum(slot_gates, axis=0, keepdims=True)
    gates_ref[...] = jnp.zeros_like(gates_ref)
    for b in range(16):
        gates_ref[b, 0:1, 0:64] = slot_gates[:, b * 64 : (b + 1) * 64]


ROUTE_AXES = ("zl", "x", "n")


def experts_step(attended, x_halves, wo, vectors, routers, prev, residual, plan, hit, grad_rows, weights):
    shifts = shifts_of(ROUTE_AXES)
    count = len(shifts)
    rows = 2 * TOK
    peers = unique([shifts, [{"c": 1}]])
    one = weights.shape[2:]

    def kernel(
        at_ref, x_ref, wo_ref, vec_ref, rc_ref, prev_ref, res_ref, plan_ref, hit_ref, gr_ref, w_hbm,
        hidden_ref, normed_ref, base_ref, table_ref, out_ref, slots_ref, dots_out, sum_ref, far_ref, far_other_ref,
        gates_s, sending, half, row_s, arrived, gates_in, w, dw, dw_in, x, xt, g, gate_col, dy, dyt, units_s, dgate_s,
        dup_s, dx_acc, out_acc, dx_s, dot_s, p_send, p_recv,
        w_sem, e_send, e_recv, g_send, g_recv, r_send, r_recv, b_send, b_recv, d_send, d_recv,
    ):
        place = coords()
        n, y, c = place["n"], place["y"], place["c"]
        me = rank_of(place, ROUTE_AXES)
        sibling = moved(place, {"c": 1})
        greet_start(place, peers)
        loads = [
            pltpu.make_async_copy(w_hbm.at[i, p], w.at[i, p], w_sem.at[i, p]) for p in range(8) for i in range(2)
        ]
        for load in loads:
            load.start()
        own_tokens = pl.ds(pl.multiple_of(n * TOK, 128), TOK)
        middle_forward(
            own_tokens, at_ref, x_ref, wo_ref, vec_ref, rc_ref, prev_ref, res_ref, plan_ref,
            hidden_ref, normed_ref, base_ref, table_ref, gates_s,
        )
        sending[...] = normed_ref[:, pl.ds(pl.multiple_of((1 - n) * HALF, 128), HALF)]
        greet_end(peers)
        swap = push(sending, half.at[n], p_send, p_recv, moved(place, {"n": 1}))
        copies = []
        for j, shift in enumerate(shifts):
            to = rank_of(place, ROUTE_AXES, shift)
            copies.append(push(gates_s.at[to], gates_in.at[me], g_send.at[j], g_recv.at[j], moved(place, shift)))
        half[n] = normed_ref[:, pl.ds(pl.multiple_of(n * HALF, 128), HALF)]
        gates_in[me] = gates_s[me]
        for source in range(8):
            for side in range(2):
                g[source * 64 : (source + 1) * 64, side * HALF : (side + 1) * HALF] = gr_ref[2 * source + side]
        swap.wait_recv()
        for e in range(4):
            span = slice(e * 256, (e + 1) * 256)
            block = dot_dims(hit_ref[span, :TOK], half[0], 1, 0) + dot_dims(hit_ref[span, TOK:], half[1], 1, 0)
            block = block.astype(bf16)
            for i in range(4):
                row_s[e * 4 + i] = block[i * 64 : (i + 1) * 64, :]
        for j, shift in enumerate(shifts):
            to = rank_of(place, ROUTE_AXES, shift)
            copies.append(push(row_s.at[to], arrived.at[me], r_send.at[j], r_recv.at[j], moved(place, shift)))
        arrived[me] = row_s[me]
        for copy in copies[:count]:
            copy.wait_recv()
        for source in range(8):
            both = gates_in[2 * source, 0:1, 0:64] + gates_in[2 * source + 1, 0:1, 0:64]
            gate_col[source * 64 : (source + 1) * 64, :] = to_column(both)
        dffn = (g[...].astype(f32) * gate_col[...]).astype(bf16)
        dy[...] = dffn
        dyt[...] = dffn.T
        dx_acc[...] = jnp.zeros_like(dx_acc)
        out_acc[...] = jnp.zeros_like(out_acc)
        for copy in copies[count:]:
            copy.wait_recv()
        for source in range(8):
            for side in range(2):
                x[source * 64 : (source + 1) * 64, side * HALF : (side + 1) * HALF] = arrived[2 * source + side]
        xt[...] = x[...].T
        sides = (slice(0, HALF), slice(HALF, D))

        def units_step(p, carry):
            gate = sum(dot_dims(x[:, s], w[i, p, 0], 1, 0) for i, s in enumerate(sides))
            up = sum(dot_dims(x[:, s], w[i, p, 1], 1, 0) for i, s in enumerate(sides))
            dunits = sum(dot_dims(dy[:, s], w[i, p, 2], 1, 0) for i, s in enumerate(sides))
            sig = 1.0 / (1.0 + jnp.exp(-gate))
            active = gate * sig
            units = (active * up).astype(bf16)
            slope = sig * (1.0 + gate * (1.0 - sig))
            dgate = (dunits * up * slope).astype(bf16)
            dup = (dunits * active).astype(bf16)
            units_s[p], dgate_s[p], dup_s[p] = units, dgate, dup
            for i, s in enumerate(sides):
                out_acc[:, s] += dot_dims(units, w[i, p, 2], 1, 1)
                dx_acc[:, s] += dot_dims(dgate, w[i, p, 0], 1, 1) + dot_dims(dup, w[i, p, 1], 1, 1)
            return carry

        for load in loads:
            load.wait()
        lax.fori_loop(0, 8, units_step, 0)
        dot_s[...] = jnp.zeros_like(dot_s)
        for source in range(8):
            span = slice(source * 64, (source + 1) * 64)
            for side in range(2):
                dx_s[2 * source + side] = dx_acc[span, sides[side]].astype(bf16)
        back = []
        for j, shift in enumerate(shifts):
            to = rank_of(place, ROUTE_AXES, shift)
            back.append(push(dx_s.at[to], slots_ref.at[me], b_send.at[j], b_recv.at[j], moved(place, shift)))
        for source in range(8):
            span = slice(source * 64, (source + 1) * 64)
            dots = jnp.sum(g[span, :].astype(f32) * out_acc[span, :], axis=1, keepdims=True)
            dot_s[source, 0:1, 0:64] = to_row(dots)
        for j, shift in enumerate(shifts):
            to = rank_of(place, ROUTE_AXES, shift)
            back.append(push(dot_s.at[to // 2], dots_out.at[me], d_send.at[j], d_recv.at[j], moved(place, shift)))
        slots_ref[me] = dx_s[me]
        dots_out[me] = dot_s[me // 2]
        for source in range(8):
            span = slice(source * 64, (source + 1) * 64)
            for side in range(2):
                out_ref[2 * source + side] = (out_acc[span, sides[side]] * gate_col[span, :]).astype(bf16)

        grad_copies = {}
        for core in (1 - c, c):
            for d in (2, 1, 3, 0):
                p = 2 * lax.rem(y + d, 4) + core
                for i, s in enumerate(sides):
                    dw[i, p, 0] = dot_dims(xt[s, :], dgate_s[p], 1, 0).astype(bf16)
                    dw[i, p, 1] = dot_dims(xt[s, :], dup_s[p], 1, 0).astype(bf16)
                    dw[i, p, 2] = dot_dims(dyt[s, :], units_s[p], 1, 0).astype(bf16)
                    if core is not c:
                        grad_copies[d, i] = push(
                            dw.at[i, p], dw_in.at[d, i], e_send.at[d, i], e_recv.at[d, i], sibling
                        )
        for d in (2, 1, 3, 0):
            totals = []
            for i in range(2):
                grad_copies[d, i].wait_recv()
                total = dw[i, 2 * lax.rem(y + d, 4) + c].astype(f32) + dw_in[d, i].astype(f32)
                totals.append(total.astype(bf16))
            if d == 2:
                far_ref[...] = jnp.where(n == 0, totals[0], totals[1])
                far_other_ref[...] = jnp.where(n == 0, totals[1], totals[0])
            else:
                sum_ref[(d + 1) // 2, 0], sum_ref[(d + 1) // 2, 1] = totals
        for copy in back:
            copy.wait_recv()
        for copy in copies + back + list(grad_copies.values()):
            copy.wait_send()
        swap.wait_send()

    route = pltpu.SemaphoreType.DMA((count,))
    return pl.pallas_call(
        kernel,
        out_shape=[
            shape_of((TOK, D), f32),
            shape_of((TOK, D), bf16),
            shape_of((2, TOK, HALF), bf16),
            shape_of((TOK, 128), f32),
            shape_of((16, 64, HALF), bf16),
            shape_of((16, 64, HALF), bf16),
            shape_of((16, 8, 128), f32),
            shape_of((3, 2) + one, bf16),
            shape_of(one, bf16),
            shape_of(one, bf16),
        ],
        in_specs=in_vmem(10) + [pl.BlockSpec(memory_space=pl.ANY)],
        out_specs=in_vmem(10),
        scratch_shapes=[
            pltpu.VMEM((16, 8, 128), f32),
            pltpu.VMEM((TOK, HALF), bf16),
            pltpu.VMEM((2, TOK, HALF), bf16),
            pltpu.VMEM((16, 64, HALF), bf16),
            pltpu.VMEM((16, 64, HALF), bf16),
            pltpu.VMEM((16, 8, 128), f32),
            pltpu.VMEM(weights.shape, bf16),
            pltpu.VMEM(weights.shape, bf16),
            pltpu.VMEM((4, 2) + one, bf16),
            pltpu.VMEM((rows, D), bf16),
            pltpu.VMEM((D, rows), bf16),
            pltpu.VMEM((rows, D), bf16),
            pltpu.VMEM((rows, 1), f32),
            pltpu.VMEM((rows, D), bf16),
            pltpu.VMEM((D, rows), bf16),
            pltpu.VMEM((8, rows, 256), bf16),
            pltpu.VMEM((8, rows, 256), bf16),
            pltpu.VMEM((8, rows, 256), bf16),
            pltpu.VMEM((rows, D), f32),
            pltpu.VMEM((rows, D), f32),
            pltpu.VMEM((16, 64, HALF), bf16),
            pltpu.VMEM((8, 8, 128), f32),
            pltpu.SemaphoreType.DMA,
            pltpu.SemaphoreType.DMA,
            pltpu.SemaphoreType.DMA((2, 8)),
            pltpu.SemaphoreType.DMA((4, 2)),
            pltpu.SemaphoreType.DMA((4, 2)),
        ]
        + [route] * 8,
        compiler_params=comm_params(6),
        name="experts_step",
    )(attended, x_halves, wo, vectors, routers, prev, residual, plan, hit, grad_rows, weights)


def middle_backward(slot_grads, hit, g_halves, hidden, normed, table, vectors, routers, dots, plan, prev, residual, wo):
    def kernel(
        rows_ref, hit_ref, g_ref, hidden_ref, normed_ref, table_ref, vec_ref, rc_ref, dots_ref, plan_ref, prev_ref,
        res_ref, wo_ref, hg_ref, og_ref, heads_ref, small_ref, gprev_ref, dn, row, sending, other, p_send, p_recv,
    ):
        place = coords()
        n = place["n"]
        neighbour = [{"n": 1}]
        greet_start(place, neighbour)
        rows = rows_ref[...].reshape(EXPERTS * CAP, HALF)
        theirs = hit_ref[:, pl.ds(pl.multiple_of((1 - n) * TOK, 128), TOK)]
        sending[...] = dot_dims(theirs, rows, 0, 0).astype(bf16)
        greet_end(neighbour)
        swap = push(sending, other, p_send, p_recv, moved(place, {"n": 1}))
        mine = hit_ref[:, pl.ds(pl.multiple_of(n * TOK, 128), TOK)]
        dn[:, pl.ds(pl.multiple_of(n * HALF, 128), HALF)] = dot_dims(mine, rows, 0, 0)
        own_tokens = pl.ds(pl.multiple_of(n * TOK, 128), TOK)
        for b in range(16):
            row[:, b * 64 : (b + 1) * 64] = dots_ref[b, 0:1, 0:64]
        table = table_ref[...]
        val = {name: column(table, name) for name in SCALARS}
        raw = table_ref[:, RAW : RAW + 16]
        g = jnp.concatenate([g_ref[0], g_ref[1]], axis=1).astype(f32)
        hidden = hidden_ref[...]
        gain = vector_rows(vec_ref, 1, 1)
        const = vector_rows(vec_ref, 2, 2)
        weighted = hidden * gain
        normed = normed_ref[...].astype(f32)
        slot = lax.broadcasted_iota(jnp.int32, (TOK, EXPERTS * CAP), 1)
        e0, e1 = plan_ref[own_tokens, 0:1], plan_ref[own_tokens, 1:2]
        dots = row[...]

        def total(array):
            return jnp.sum(array, axis=1, keepdims=True)

        dot_self = total(g * normed)
        dot_vec = [total(g * const[j : j + 1]) for j in range(2)]
        const_dots = [
            val["a00"] * dot_self + val["a01"] * dot_vec[0],
            val["a10"] * dot_self + val["a11"] * dot_vec[1],
        ]

        def gate_dot(expert, places):
            result = total(jnp.where(slot == places, dots, 0.0))
            result = result + jnp.where(expert == EXPERTS + 1, dot_self, 0.0)
            for j in range(2):
                result = result + jnp.where(expert == EXPERTS + 2 + j, const_dots[j], 0.0)
            return result

        d0, d1 = gate_dot(e0, plan_ref[own_tokens, 2:3]), gate_dot(e1, plan_ref[own_tokens, 3:4])
        mean = val["gate0"] * d0 + val["gate1"] * d1
        route = lax.broadcasted_iota(jnp.int32, (TOK, 16), 1)
        grads = jnp.where(route == e0, val["gate0"] * (d0 - mean), 0.0)
        grads = grads + jnp.where(route == e1, val["gate1"] * (d1 - mean), 0.0)
        logits_grad = grads[:, :ROUTES]
        for j in range(2):
            first, second = val["a%d0" % j], val["a%d1" % j]
            weight = val["cw%d" % j]
            da, db = weight * dot_self, weight * dot_vec[j]
            middle = first * da + second * db
            grads = jnp.where(route == ROUTES + 2 * j, first * (da - middle), grads)
            grads = jnp.where(route == ROUTES + 2 * j + 1, second * (db - middle), grads)
        inv = val["inv"]
        scaled_grads = inv * grads
        weighted_grad = exact_dims(scaled_grads, router_table(rc_ref), 1, 1)
        swap.wait_recv()
        dn[:, pl.ds(pl.multiple_of((1 - n) * HALF, 128), HALF)] = other[...].astype(f32)
        normed_grad = dn[...] + val["self"] * g
        inv_grad = total(normed_grad * weighted) + total(grads * raw)
        small_ref[...] = jnp.zeros_like(small_ref)
        small_ref[0:16, :D] = exact_dims(scaled_grads, weighted, 0, 0)
        small_ref[16:17, :D] = jnp.sum(val["vec0"] * g, axis=0, keepdims=True)
        small_ref[17:18, :D] = jnp.sum(val["vec1"] * g, axis=0, keepdims=True)
        small_ref[18:19, :D] = jnp.sum(normed_grad * hidden * inv + weighted_grad * hidden, axis=0, keepdims=True)
        small_ref[0:ROUTES, D : D + ROUTES] = exact_dims(prev_ref[:, own_tokens], logits_grad, 1, 0)
        gprev_ref[...] = jnp.zeros_like(gprev_ref)
        gprev_ref[0, 0:ROUTES, :] = exact_dims(res_ref[...].astype(f32), logits_grad, 1, 1)
        hidden_grad = (
            g
            + normed_grad * inv * gain
            + weighted_grad * gain
            - (inv_grad * (inv * inv * inv) / D) * hidden
        )
        hg_ref[...] = hidden_grad
        out_grad = hidden_grad.astype(bf16)
        og_ref[...] = out_grad
        for y in range(4):
            heads_ref[y] = dot_dims(wo_ref[y * 192 : (y + 1) * 192, :], out_grad, 1, 1).astype(bf16)
        swap.wait_send()

    return pl.pallas_call(
        kernel,
        out_shape=[
            shape_of((TOK, D), f32),
            shape_of((TOK, D), bf16),
            shape_of((4, 192, TOK), bf16),
            shape_of((24, D + 128), f32),
            shape_of((1, 16, TOK), f32),
        ],
        in_specs=in_vmem(13),
        out_specs=in_vmem(5),
        scratch_shapes=[
            pltpu.VMEM((TOK, D), f32),
            pltpu.VMEM((1, EXPERTS * CAP), f32),
            pltpu.VMEM((TOK, HALF), bf16),
            pltpu.VMEM((TOK, HALF), bf16),
            pltpu.SemaphoreType.DMA,
            pltpu.SemaphoreType.DMA,
        ],
        compiler_params=comm_params(7),
        name="middle_backward",
    )(slot_grads, hit, g_halves, hidden, normed, table, vectors, routers, dots, plan, prev, residual, wo)


def key_ids(ids_ref, place, block, tile):
    return ids_ref[(place["zl"] * 4 + place["x"]) * 8 + 2 * block + tile]


def query_ids(ids_ref, place, chunk):
    row = (place["zl"] * 4 + place["x"]) * 8 + 2 * chunk + place["c"]
    return ids_ref[row, :, pl.ds(pl.multiple_of(place["n"] * TOK, 128), TOK)]


def for_chunks(block, part, whole_chunks, partial_chunk):
    masked = [
        (block, 0, 1),
        (block, 1, jnp.minimum(part, 1)),
        (block - 1, 0, jnp.where((part == 3) & (block > 0), 1, 0)),
    ]
    for chunk, tile, times in masked:

        def body(_, carry, chunk=chunk, tile=tile):
            partial_chunk(chunk, tile)
            return carry

        if isinstance(times, int):
            partial_chunk(chunk, tile)
        else:
            lax.fori_loop(0, times, body, 0)
    yield
    lax.fori_loop(block + 1, 4, lambda j, carry: (whole_chunks(j), carry)[1], 0)
    yield


def attend(queries, pairs, grad_rows, block_ids):
    route_shifts = shifts_of(ROUTE_AXES)
    peers = unique([shifts_of(("y",)), [{"n": 1}], [{"c": 1}], route_shifts])

    def kernel(
        q_in, kv_in, rows_in, ids_ref, at_out, q_out, kv_out, of_ref, lse_ref, rows_out,
        q_now, o_now, top_s, total_s, acc_s,
        q_send, q_recv, y_send, y_recv, n_send, n_recv, c_send, c_recv, o_send, o_recv, r_send, r_recv,
    ):
        place = coords()
        y, c, n = place["y"], place["c"], place["n"]
        part = 2 * c + n
        partner, sibling = moved(place, {"n": 1}), moved(place, {"c": 1})
        me = rank_of(place, ROUTE_AXES)
        kv_out[y, c, n] = kv_in[y]
        q_now[y] = q_in[y]
        greet(place, peers)
        query_copies, row_copies = [], []
        pair_copies, across, beside, onward = {}, {}, {}, {}

        def spread(d):
            spot = kv_out.at[lax.rem(y + 4 - d, 4), c, n]
            across[d] = push(spot, spot, n_send.at[d], n_recv.at[d], partner)
            beside[d] = push(spot, spot, c_send.at[0, d], c_recv.at[0, d], sibling)

        def pass_on(d):
            across[d].wait_recv()
            spot = kv_out.at[lax.rem(y + 4 - d, 4), c, 1 - n]
            onward[d] = push(spot, spot, c_send.at[1, d], c_recv.at[1, d], sibling)

        def send_pairs(d):
            target = lax.rem(y + d, 4)
            pair_copies[d] = push(
                kv_in.at[target], kv_out.at[y, c, n], y_send.at[d], y_recv.at[d], moved(place, {"y": d})
            )

        def send_rows():
            for j, shift in enumerate(route_shifts):
                to = rank_of(place, ROUTE_AXES, shift)
                row_copies.append(
                    push(rows_in.at[to], rows_out.at[me], r_send.at[j], r_recv.at[j], moved(place, shift))
                )
            rows_out[me] = rows_in[me]

        send_pairs(1)
        send_pairs(3)
        spread(0)
        for d in (1, 3, 2):
            target = lax.rem(y + d, 4)
            query_copies.append(
                push(q_in.at[target], q_now.at[y], q_send.at[d], q_recv.at[d], moved(place, {"y": d}))
            )
        send_pairs(2)
        top_s[...] = jnp.full_like(top_s, -1e30)
        total_s[...] = jnp.zeros_like(total_s)
        acc_s[...] = jnp.zeros_like(acc_s)
        q_out[...] = jnp.zeros_like(q_out)
        pass_on(0)
        for d in (1, 3):
            pair_copies[d].wait_recv()
            spread(d)
        for copy in query_copies:
            copy.wait_recv()
        for j in range(4):
            for h in range(3):
                q_out[j, h, :HEAD_DIM, :] = q_now[j, h * HEAD_DIM : (h + 1) * HEAD_DIM, :] * 0.125

        def update(j, block, tiles, masked):
            if masked:
                allowed = [to_column(key_ids(ids_ref, place, block, t)) <= query_ids(ids_ref, place, j) for t in tiles]
            k_tiles = {}
            scores = {}
            for h in range(3):
                lanes = slice(h * 128, (h + 1) * 128)
                for t in tiles:
                    k_tiles[h, t] = kv_out[block, t, :, :, lanes].reshape(KT, 128)
                    scores[h, t] = dot_dims(k_tiles[h, t], q_out[j, h], 1, 0)
            state = []
            for h in range(3):
                mine = [scores[h, t] for t in tiles]
                if masked:
                    mine = [jnp.where(a, s, -1e30) for a, s in zip(allowed, mine)]
                old = top_s[j, h]
                top = old
                for s in mine:
                    top = jnp.maximum(top, jnp.max(s, axis=0, keepdims=True))
                decay = jnp.exp(old - top)
                total = total_s[j, h] * decay
                acc = acc_s[j, h] * decay
                for t, s in zip(tiles, mine):
                    p = jnp.exp(s - top)
                    total = total + jnp.sum(p, axis=0, keepdims=True)
                    acc = acc + dot_dims(k_tiles[h, t], p.astype(bf16), 0, 0)
                state.append((top, total, acc))
            for h in range(3):
                top_s[j, h], total_s[j, h], acc_s[j, h] = state[h]

        def second_pairs():
            pair_copies[2].wait_recv()
            spread(2)
            pass_on(1)
            send_rows()

        between = {0: second_pairs, 1: lambda: pass_on(3), 3: lambda: pass_on(2), 2: lambda: None}
        for d in (0, 1, 3, 2):
            beside[d].wait_recv()
            onward[d].wait_recv()
            block = lax.rem(y + 4 - d, 4)
            halves = for_chunks(
                block,
                part,
                lambda j, block=block: update(j, block, (0, 1), False),
                lambda j, t, block=block: update(j, block, (t,), True),
            )
            next(halves)
            between[d]()
            next(halves)

        out_copies = []
        for d in (2, 1, 3, 0):
            j = lax.rem(y + d, 4)
            for h in range(3):
                total = total_s[j, h]
                span = slice(h * HEAD_DIM, (h + 1) * HEAD_DIM)
                out = acc_s[j, h, HEAD_DIM:, :] * (1.0 / total)
                of_ref[j, span, :] = out
                o_now[j, span, :] = out.astype(bf16)
                lse_ref[j, h] = top_s[j, h] + jnp.log(total)
            if d:
                out_copies.append(
                    push(o_now.at[j], at_out.at[y], o_send.at[d], o_recv.at[d], moved(place, {"y": d}))
                )
            else:
                at_out[y] = o_now[y]
        for copy in out_copies + row_copies:
            copy.wait_recv()
        sent = query_copies + list(pair_copies.values()) + row_copies + out_copies
        for copy in sent + list(across.values()) + list(beside.values()) + list(onward.values()):
            copy.wait_send()

    four = pltpu.SemaphoreType.DMA((4,))
    return pl.pallas_call(
        kernel,
        out_shape=[
            shape_of((4, 192, TOK), bf16),
            shape_of((4, 3, 128, TOK), bf16),
            shape_of((4, 2, 2, TOK, HALF), bf16),
            shape_of((4, 192, TOK), f32),
            shape_of((4, 3, 1, TOK), f32),
            shape_of(grad_rows.shape, bf16),
        ],
        in_specs=in_vmem(4),
        out_specs=in_vmem(6),
        scratch_shapes=[
            pltpu.VMEM((4, 192, TOK), bf16),
            pltpu.VMEM((4, 192, TOK), bf16),
            pltpu.VMEM((4, 3, 1, TOK), f32),
            pltpu.VMEM((4, 3, 1, TOK), f32),
            pltpu.VMEM((4, 3, 128, TOK), f32),
            four,
            four,
            four,
            four,
            four,
            four,
            pltpu.SemaphoreType.DMA((2, 4)),
            pltpu.SemaphoreType.DMA((2, 4)),
            four,
            four,
            pltpu.SemaphoreType.DMA((len(route_shifts),)),
            pltpu.SemaphoreType.DMA((len(route_shifts),)),
        ],
        compiler_params=comm_params(2),
        name="attend",
    )(queries, pairs, grad_rows, block_ids)


def attend_backward(grads, queries, pairs, attended, logs, block_ids, out_rows, small, weight_sums, swaps_in):
    extra = len(swaps_in)
    route_shifts = shifts_of(ROUTE_AXES)
    peers = unique([shifts_of(("y",)), shifts_of(("x",)), shifts_of(("z",)), [{"c": 1}], route_shifts])
    turns = ("c", "x", "y", "z")
    order = (1, 3, 2, 0)

    def kernel(*refs):
        g_in, q_ref, kv_ref, of_ref, lse_ref, ids_ref, rows_in, small_in, sums_ref = refs[:9]
        ins = refs[9 : 9 + extra]
        dq_out, dkv_out, rows_out, small_out, sum_out, sum_other = refs[9 + extra : 15 + extra]
        swapped = refs[15 + extra : 15 + 2 * extra]
        (
            g_now, g_pad, delta_s, dq_acc, dq_now, acc, own_sum, to_sibling, from_sibling, to_other, from_other, kept, ready,
            small_now, small_in_flight, g_send, g_recv, c_send, c_recv, n_send, n_recv, y_send, y_recv,
            q_send, q_recv, r_send, r_recv, s_send, s_recv, p_send, p_recv, sum_in, w_send, w_recv, own_sem,
        ) = refs[15 + 2 * extra :]
        place = coords()
        y, c, n = place["y"], place["c"], place["n"]
        part = 2 * c + n
        partner, sibling = moved(place, {"n": 1}), moved(place, {"c": 1})
        me = rank_of(place, ROUTE_AXES)
        greet(place, peers)
        grad_copies, row_copies = [], []
        for d in (2, 1, 3):
            target = lax.rem(y + d, 4)
            grad_copies.append(
                push(g_in.at[target], g_now.at[y], g_send.at[d], g_recv.at[d], moved(place, {"y": d}))
            )
        g_now[y] = g_in[y]
        small_now[0] = small_in[...]

        def small_start(turn):
            axis = turns[turn]
            return [
                push(
                    small_now.at[turn],
                    small_in_flight.at[turn, d],
                    s_send.at[turn, d],
                    s_recv.at[turn, d],
                    moved(place, {axis: d + 1}),
                )
                for d in range(SIZES[axis] - 1)
            ]

        def small_end(turn, copies):
            total = small_now[turn]
            for d, copy in enumerate(copies):
                copy.wait_recv()
                total = total + small_in_flight[turn, d]
            if turn < 3:
                small_now[turn + 1] = total
            else:
                small_out[...] = total

        small_copies = [small_start(0)]
        swaps = swap_start(place, swaps_in, ins, swapped, p_send, p_recv)
        for j, shift in enumerate(route_shifts):
            to = rank_of(place, ROUTE_AXES, shift)
            row_copies.append(
                push(rows_in.at[to], rows_out.at[me], r_send.at[j], r_recv.at[j], moved(place, shift))
            )
        rows_out[me] = rows_in[me]
        dq_acc[...] = jnp.zeros_like(dq_acc)
        g_pad[...] = jnp.zeros_like(g_pad)
        for copy in grad_copies:
            copy.wait_recv()
        weight_copies = []
        for d in (1, 3):
            for i in range(2):
                weight_copies.append(
                    push(
                        sums_ref.at[(d + 1) // 2, i], sum_in.at[d // 2, i], w_send.at[d // 2, i], w_recv.at[d // 2, i],
                        moved(place, {"y": d}),
                    )
                )
        own_load = pltpu.make_async_copy(sums_ref.at[0], own_sum, own_sem)
        own_load.start()
        for j in range(4):
            inner = g_now[j].astype(f32) * of_ref[j]
            for h in range(3):
                span = slice(h * HEAD_DIM, (h + 1) * HEAD_DIM)
                g_pad[j, h, HEAD_DIM:, :] = g_now[j, span, :]
                delta_s[j, h] = jnp.sum(inner[span, :], axis=0, keepdims=True)

        def update(j, block, tiles, masked):
            if masked:
                allowed = {t: to_column(key_ids(ids_ref, place, block, t)) <= query_ids(ids_ref, place, j) for t in tiles}
            places = [(t, h) for t in tiles for h in range(3)]
            k_tiles, scores, grads, both, dq = {}, {}, {}, {}, {}
            for t, h in places:
                k = kv_ref[block, t, :, :, h * 128 : (h + 1) * 128].reshape(KT, 128)
                k_tiles[t, h] = k
                scores[t, h] = dot_dims(k, q_ref[j, h], 1, 0)
                grads[t, h] = dot_dims(k, g_pad[j, h], 1, 0)
            for t, h in places:
                p = jnp.exp(scores[t, h] - lse_ref[j, h])
                if masked:
                    p = jnp.where(allowed[t], p, 0.0)
                ds = (p * (grads[t, h] - delta_s[j, h])).astype(bf16)
                both[t, h] = dot_dims(ds, q_ref[j, h], 1, 1) + dot_dims(p.astype(bf16), g_pad[j, h], 1, 1)
                more = dot_dims(k_tiles[t, h], ds, 0, 0)
                dq[h] = dq[h] + more if h in dq else more
            for t, h in places:
                acc[t, :, :, h * 128 : (h + 1) * 128] += both[t, h].reshape(2, TOK, 128)
            for h in range(3):
                dq_acc[j, h] += dq[h]

        beside, across, homeward = {}, {}, []

        def send_beside(d):
            to_sibling[d] = acc[1 - c].astype(bf16)
            beside[d] = push(to_sibling.at[d], from_sibling.at[d], c_send.at[d], c_recv.at[d], sibling)
            kept[d] = acc[c]

        def send_across(d):
            beside[d].wait_recv()
            to_other[d] = (kept[d, 1 - n] + from_sibling[d, 1 - n].astype(f32)).astype(bf16)
            across[d] = push(to_other.at[d], from_other.at[d], n_send.at[d], n_recv.at[d], partner)

        def send_home(d):
            across[d].wait_recv()
            total = kept[d, n] + from_sibling[d, n].astype(f32) + from_other[d].astype(f32)
            if d:
                ready[d] = total.astype(bf16)
                homeward.append(
                    push(ready.at[d], dkv_out.at[y], y_send.at[d], y_recv.at[d], moved(place, {"y": d}))
                )
            else:
                dkv_out[y] = total.astype(bf16)

        for step, d in enumerate(order):
            block = lax.rem(y + d, 4)
            acc[...] = jnp.zeros_like(acc)
            halves = for_chunks(
                block,
                part,
                lambda j, block=block: update(j, block, (0, 1), False),
                lambda j, t, block=block: update(j, block, (t,), True),
            )
            next(halves)
            if step:
                send_across(order[step - 1])
                small_end(step - 1, small_copies[step - 1])
                small_copies.append(small_start(step))
            if step > 1:
                send_home(order[step - 2])
            next(halves)
            send_beside(d)
        query_copies = []
        for d in (2, 1, 3, 0):
            j = lax.rem(y + d, 4)
            grad = jnp.concatenate([dq_acc[j, h, :HEAD_DIM, :] for h in range(3)], axis=0)
            grad = (grad * 0.125).astype(bf16)
            if d:
                dq_now[j] = grad
                query_copies.append(
                    push(dq_now.at[j], dq_out.at[y], q_send.at[d], q_recv.at[d], moved(place, {"y": d}))
                )
            else:
                dq_out[y] = grad
        send_home(order[2])
        send_across(order[3])
        small_end(3, small_copies[3])
        send_home(order[3])
        for copy in weight_copies:
            copy.wait_recv()
        own_load.wait()
        totals = []
        for i in range(2):
            total = own_sum[i].astype(f32) + sum_in[0, i].astype(f32) + sum_in[1, i].astype(f32)
            totals.append(total.astype(bf16))
        sum_out[...] = jnp.where(n == 0, totals[0], totals[1])
        sum_other[...] = jnp.where(n == 0, totals[1], totals[0])
        for copy in homeward + query_copies + row_copies + swaps:
            copy.wait_recv()
        sent = grad_copies + row_copies + swaps + query_copies + homeward + weight_copies
        for copy in sent + list(beside.values()) + list(across.values()):
            copy.wait_send()
        for copies in small_copies:
            for copy in copies:
                copy.wait_send()

    four = pltpu.SemaphoreType.DMA((4,))
    return pl.pallas_call(
        kernel,
        out_shape=[
            shape_of((4, 192, TOK), bf16),
            shape_of((4, TOK, HALF), bf16),
            shape_of(out_rows.shape, bf16),
            shape_of(small.shape, f32),
            shape_of(weight_sums.shape[2:], bf16),
            shape_of(weight_sums.shape[2:], bf16),
        ]
        + swap_shapes(swaps_in),
        in_specs=in_vmem(8) + [pl.BlockSpec(memory_space=pl.ANY)] + in_vmem(extra),
        out_specs=in_vmem(6 + extra),
        scratch_shapes=[
            pltpu.VMEM((4, 192, TOK), bf16),
            pltpu.VMEM((4, 3, 128, TOK), bf16),
            pltpu.VMEM((4, 3, 1, TOK), f32),
            pltpu.VMEM((4, 3, 128, TOK), f32),
            pltpu.VMEM((4, 192, TOK), bf16),
            pltpu.VMEM((2, 2, TOK, HALF), f32),
            pltpu.VMEM(weight_sums.shape[1:], bf16),
            pltpu.VMEM((4, 2, TOK, HALF), bf16),
            pltpu.VMEM((4, 2, TOK, HALF), bf16),
            pltpu.VMEM((4, TOK, HALF), bf16),
            pltpu.VMEM((4, TOK, HALF), bf16),
            pltpu.VMEM((4, 2, TOK, HALF), f32),
            pltpu.VMEM((4, TOK, HALF), bf16),
            pltpu.VMEM((4,) + small.shape, f32),
            pltpu.VMEM((4, 3) + small.shape, f32),
        ]
        + [four] * 10
        + [pltpu.SemaphoreType.DMA((len(route_shifts),))] * 2
        + [pltpu.SemaphoreType.DMA((4, 3))] * 2
        + [pltpu.SemaphoreType.DMA((extra,))] * 2
        + [pltpu.VMEM((2,) + weight_sums.shape[1:], bf16)]
        + [pltpu.SemaphoreType.DMA((2, 2))] * 2
        + [pltpu.SemaphoreType.DMA],
        compiler_params=comm_params(3),
        name="attend_backward",
    )(
        grads, queries, pairs, attended, logs, block_ids, out_rows, small, weight_sums,
        *[a for a, _ in swaps_in],
    )


def project_backward(
    dq_ref, dkv_ref, pq_ref, proj_ref, inv_ref, scaled_ref, wq_ref, x_ref, vec_ref, hg_ref, at_ref, og_ref,
    pa, pb, pc, grad_ref, gain_ref, dw_s, dwo_s,
):
    inv = inv_ref[...]
    scaled = scaled_ref[...]
    dscaled = jnp.zeros((TOK, D), f32)
    dinv = jnp.zeros((TOK, 192), f32)
    dinv_row = jnp.zeros((1, TOK), f32)
    inv_row = to_row(inv)
    for s in range(3):
        for y in range(4):
            first = s * D + y * 192
            if s == 0:
                d = dq_ref[y].astype(f32)
                dinv_row = dinv_row + jnp.sum(d * pq_ref[y], axis=0, keepdims=True)
                dproject = (inv_row * d).astype(bf16)
                dscaled = dscaled + dot_dims(dproject, wq_ref[first : first + 192, :], 0, 0)
                dw_s[first : first + 192, :] = dot_dims(dproject, scaled, 1, 0)
                continue
            d = jnp.concatenate(
                [
                    dkv_ref[y, :, h * 128 + (s - 1) * HEAD_DIM : h * 128 + s * HEAD_DIM]
                    for h in range(3)
                ],
                axis=1,
            ).astype(f32)
            dinv = dinv + d * proj_ref[(s - 1) * 4 + y]
            dproject = (inv * d).astype(bf16)
            dscaled = dscaled + dot_dims(dproject, wq_ref[first : first + 192, :], 1, 0)
            dw_s[first : first + 192, :] = dot_dims(dproject, scaled, 0, 0)
    for y in range(4):
        dwo_s[y * 192 : (y + 1) * 192, :] = dot_dims(at_ref[y], og_ref[...], 1, 0)
    for w, cols, spots in blocks_of_weights():
        pa[spots[0]] = dw_s[w * 36 : w * 36 + 16, cols].astype(bf16)
        pb[spots[1]] = dw_s[w * 36 + 16 : w * 36 + 32, cols].astype(bf16)
        pc[spots[2]] = jnp.concatenate(
            [dw_s[w * 36 + 32 : w * 36 + 36, cols], dwo_s[w * 12 : w * 12 + 12, cols]], axis=0
        ).astype(bf16)
    x = jnp.concatenate([x_ref[0], x_ref[1]], axis=1).astype(f32)
    gain = jnp.concatenate([vec_ref[0, 0:1], vec_ref[1, 0:1]], axis=1).astype(f32)
    gain_ref[0] = jnp.zeros_like(gain_ref[0])
    gain_ref[0, 0:1, :] = jnp.sum(dscaled * x, axis=0, keepdims=True)
    dinv = jnp.sum(dinv, axis=1, keepdims=True) + to_column(dinv_row)
    grad = hg_ref[...] + dscaled * gain - (dinv * (inv * inv * inv) / D) * x
    for half in range(2):
        grad_ref[half] = grad[:, half * HALF : (half + 1) * HALF].astype(bf16)


def scatter_sums(given):
    swaps_in = [(shape_of((2, TOK, HALF), bf16), 1)]
    small = shape_of((8, D), f32)
    extra = len(swaps_in)
    peers = unique([shifts_of((a,)) for a in ("x", "y", "z", "c")])
    turns = ("c", "x", "y", "z")
    count = len(given)

    def kernel(*refs):
        block_out, small_out = refs[count : count + 2]
        swapped = refs[count + 2 : count + 2 + extra]
        rest = refs[count + 2 + extra :]
        parts_in, grad_s, dw_s, dwo_s = rest[:3], rest[3], rest[4], rest[5]
        rest = rest[6:]
        from_sibling, sum_three, sum_two, sum_one = rest[0:3], rest[3:6], rest[6:9], rest[9:12]
        in_three, in_two, in_one = rest[12:15], rest[15:18], rest[18:21]
        (
            small_now,
            small_in_flight,
            c_send,
            c_recv,
            send,
            recv,
            s_send,
            s_recv,
            p_send,
            p_recv,
        ) = rest[21:]
        place = coords()
        core = place["c"]
        ins = (grad_s,)
        greet_start(place, peers)
        project_backward(*refs[:count], *parts_in, grad_s, small_now, dw_s, dwo_s)
        greet_end(peers)
        beside = []
        for j in range(4):
            for k in range(3):
                third = lax.rem(place[ORDERS[k][2]] + (j + 1), 4)
                beside.append(
                    push(
                        parts_in[k].at[1 - core, third],
                        from_sibling[k].at[third],
                        c_send.at[k, j],
                        c_recv.at[k, j],
                        moved(place, {"c": 1}),
                    )
                )

        def small_start(turn):
            axis = turns[turn]
            return [
                push(
                    small_now.at[turn],
                    small_in_flight.at[turn, d],
                    s_send.at[turn, d],
                    s_recv.at[turn, d],
                    moved(place, {axis: d + 1}),
                )
                for d in range(SIZES[axis] - 1)
            ]

        def small_end(turn, copies):
            total = small_now[turn]
            for d, copy in enumerate(copies):
                copy.wait_recv()
                total = total + small_in_flight[turn, d]
            if turn < 3:
                small_now[turn + 1] = total
            else:
                small_out[...] = total

        small_copies = [small_start(0)]
        threes = [[] for _ in range(3)]
        for j in range(4):
            for k in range(3):
                third = lax.rem(place[ORDERS[k][2]] + (j + 1), 4)
                beside[j * 3 + k].wait_recv()
                sum_three[k][third] = (
                    parts_in[k][core, third].astype(f32) + from_sibling[k][third].astype(f32)
                ).astype(bf16)
                if j < 3:
                    threes[k].append(
                        push(
                            sum_three[k].at[third],
                            in_three[k].at[j],
                            send.at[k, 0, j],
                            recv.at[k, 0, j],
                            moved(place, {ORDERS[k][2]: j + 1}),
                        )
                    )
        swaps = swap_start(place, swaps_in, ins, swapped, p_send, p_recv)
        small_end(0, small_copies[0])
        small_copies.append(small_start(1))
        twos = [[] for _ in range(3)]
        for k in range(3):
            for copy in threes[k]:
                copy.wait_recv()
            third = place[ORDERS[k][2]]
            total = sum_three[k][third].astype(f32)
            for j in range(3):
                total = total + in_three[k][j].astype(f32)
            sum_two[k][...] = total.astype(bf16)
            for j in range(3):
                second = lax.rem(place[ORDERS[k][1]] + (j + 1), 4)
                twos[k].append(
                    push(
                        sum_two[k].at[second],
                        in_two[k].at[j],
                        send.at[k, 1, j],
                        recv.at[k, 1, j],
                        moved(place, {ORDERS[k][1]: j + 1}),
                    )
                )
        small_end(1, small_copies[1])
        small_copies.append(small_start(2))
        ones = [[] for _ in range(3)]
        for k in range(3):
            for copy in twos[k]:
                copy.wait_recv()
            second = place[ORDERS[k][1]]
            total = sum_two[k][second].astype(f32)
            for j in range(3):
                total = total + in_two[k][j].astype(f32)
            sum_one[k][...] = total.astype(bf16)
            for j in range(3):
                first = lax.rem(place[ORDERS[k][0]] + (j + 1), 4)
                ones[k].append(
                    push(
                        sum_one[k].at[first],
                        in_one[k].at[j],
                        send.at[k, 2, j],
                        recv.at[k, 2, j],
                        moved(place, {ORDERS[k][0]: j + 1}),
                    )
                )
        small_end(2, small_copies[2])
        small_copies.append(small_start(3))
        for k in range(3):
            for copy in ones[k]:
                copy.wait_recv()
            first = place[ORDERS[k][0]]
            total = sum_one[k][first].astype(f32)
            for j in range(3):
                total = total + in_one[k][j].astype(f32)
            block_out[k * PART : (k + 1) * PART, :] = total
        small_end(3, small_copies[3])
        for copy in swaps:
            copy.wait_recv()
        for copy in beside + swaps:
            copy.wait_send()
        for k in range(3):
            for copy in threes[k] + twos[k] + ones[k]:
                copy.wait_send()
        for copies in small_copies:
            for copy in copies:
                copy.wait_send()

    three = pltpu.VMEM((4, 4, 4, PART, HALF), bf16)
    two = pltpu.VMEM((4, 4, PART, HALF), bf16)
    one = pltpu.VMEM((4, PART, HALF), bf16)
    return pl.pallas_call(
        kernel,
        out_shape=[shape_of((3 * PART, HALF), f32), small] + swap_shapes(swaps_in),
        in_specs=in_vmem(count),
        out_specs=in_vmem(2 + extra),
        scratch_shapes=[pltpu.VMEM((2, 4, 4, 4, PART, HALF), bf16)] * 3
        + [pltpu.VMEM((2, TOK, HALF), bf16), pltpu.VMEM((3 * D, D), f32), pltpu.VMEM((D, D), f32)]
        + [three] * 3
        + [three] * 3
        + [two] * 3
        + [one] * 3
        + [pltpu.VMEM((3, 4, 4, PART, HALF), bf16)] * 3
        + [pltpu.VMEM((3, 4, PART, HALF), bf16)] * 3
        + [pltpu.VMEM((3, PART, HALF), bf16)] * 3
        + [
            pltpu.VMEM((4,) + small.shape, f32),
            pltpu.VMEM((4, 3) + small.shape, f32),
            pltpu.SemaphoreType.DMA((3, 4)),
            pltpu.SemaphoreType.DMA((3, 4)),
            pltpu.SemaphoreType.DMA((3, 3, 3)),
            pltpu.SemaphoreType.DMA((3, 3, 3)),
            pltpu.SemaphoreType.DMA((4, 3)),
            pltpu.SemaphoreType.DMA((4, 3)),
            pltpu.SemaphoreType.DMA((extra,)),
            pltpu.SemaphoreType.DMA((extra,)),
        ],
        compiler_params=comm_params(4),
        name="scatter_sums",
    )(*given)


def finish(grad_block, gain_sum, grad_halves, small, grad_prev, expert_sums, base, out_slots, hit):
    def kernel(
        block_ref, gain_ref, halves_ref, small_ref, prev_ref, s0_ref, s1_ref, s2_ref, s3_ref, base_ref, slots_ref, hit_ref,
        layer_out, g_inputs, g_prev, g_gain_one, g_qkv, g_out, g_gain_two, g_router, g_residual, g_const, g_vec,
        g_gate, g_up, g_down,
    ):
        n = lax.axis_index("n")
        cols = pl.ds(pl.multiple_of(n * HALF, 128), HALF)
        mixture = dot_dims(hit_ref[...], slots_ref[...].reshape(EXPERTS * CAP, HALF), 0, 0)
        for side in range(2):
            span = slice(side * TOK, (side + 1) * TOK)
            layer_out[span, :] = (base_ref[side].astype(f32) + mixture[span, :]).astype(bf16)
            g_inputs[span, :] = halves_ref[side].astype(f32)
            g_prev[:, span] = prev_ref[side, :ROUTES, :]
        g_gain_one[...] = gain_ref[0:1, cols]
        block = block_ref[...]
        g_qkv[...] = block[:36, :]
        g_out[...] = block[36:48, :]
        g_router[...] = small_ref[:ROUTES, cols]
        g_const[...] = small_ref[ROUTES:16, cols]
        g_vec[...] = small_ref[16:18, cols]
        g_gain_two[...] = small_ref[18:19, cols]
        g_residual[...] = small_ref[0:ROUTES, D : D + ROUTES]
        for i, target in enumerate((g_gate, g_up, g_down)):
            total = sum(ref[i].astype(f32) for ref in (s0_ref, s1_ref, s2_ref, s3_ref))
            target[...] = total if i < 2 else total.T

    shapes = [
        shape_of((2 * TOK, HALF), bf16),
        shape_of((2 * TOK, HALF), f32),
        shape_of((ROUTES, 2 * TOK), f32),
        shape_of((1, HALF), f32),
        shape_of((36, HALF), f32),
        shape_of((12, HALF), f32),
        shape_of((1, HALF), f32),
        shape_of((ROUTES, HALF), f32),
        shape_of((ROUTES, ROUTES), f32),
        shape_of((4, HALF), f32),
        shape_of((2, HALF), f32),
        shape_of((HALF, 256), f32),
        shape_of((HALF, 256), f32),
        shape_of((256, HALF), f32),
    ]
    return pl.pallas_call(
        kernel,
        out_shape=shapes,
        in_specs=in_vmem(12),
        out_specs=in_vmem(len(shapes)),
        compiler_params=pltpu.CompilerParams(vmem_limit_bytes=VMEM_LIMIT),
        name="finish",
    )(grad_block, gain_sum, grad_halves, small, grad_prev, *expert_sums, base, out_slots, hit)


def shards(
    inputs,
    block_ids,
    expert_ids,
    prev_scores,
    gain_one,
    w_qkv,
    w_out,
    gain_two,
    w_router,
    w_residual,
    w_const,
    const_vec,
    w_gate,
    w_up,
    w_down,
    cotangent,
):
    expert_block = jnp.stack([w_gate, w_up, w_down.T])
    weights = lax.all_gather(expert_block, ("n", "y", "c"), axis=0, tiled=False).reshape(2, 8, 3, HALF, 256)

    *parts, x_halves, g_halves, vectors, routers, hit, plan, grad_rows = gather_all(
        w_qkv.T,
        w_out,
        inputs.reshape(2, TOK, HALF),
        cotangent.reshape(2, TOK, HALF),
        [gain_one[None], gain_two[None], const_vec],
        [w_router.T, w_const.T],
        expert_ids.T,
    )
    wq, wo, queries, pairs, project_q, project, scaled, inv_one = project_forward(parts, x_halves, vectors)
    blocks = block_ids.reshape(64, 1, 512)
    prev = prev_scores.T
    attended, queries, pairs, attended_f, logs, grad_rows = attend(queries, pairs, grad_rows, blocks)
    hidden, normed, base, table, out_rows, slot_grads, dots, weight_sums, far, far_other = experts_step(
        attended, x_halves, wo, vectors, routers, prev, w_residual, plan, hit, grad_rows, weights
    )
    two_on = [(i, (i + 2) % 4) for i in range(4)]
    far = lax.ppermute(far, "y", two_on)
    far_other = lax.ppermute(
        far_other, ("n", "y"), [(4 * k + i, 4 * (1 - k) + j) for k in range(2) for i, j in two_on]
    )
    hidden_grad, out_grad, heads_grad, small, grad_prev = middle_backward(
        slot_grads, hit, g_halves, hidden, normed, table, vectors, routers, dots, plan, prev, w_residual, wo
    )
    dq, dkv, out_slots, small, near, near_other, grad_prev, base = attend_backward(
        heads_grad, queries, pairs, attended_f, logs, blocks, out_rows, small, weight_sums,
        [(grad_prev, 2), (base, 1)],
    )
    near_other = lax.ppermute(near_other, "n", [(0, 1), (1, 0)])
    grad_block, gain_sum, grad_halves = scatter_sums(
        [
            dq, dkv, project_q, project, inv_one, scaled, wq, x_halves, vectors, hidden_grad, attended, out_grad,
        ]
    )
    outputs = finish(
        grad_block, gain_sum, grad_halves, small, grad_prev, (near, near_other, far, far_other), base, out_slots, hit
    )
    turned = {2, 4, 7, 9}
    return tuple(
        out.reshape(HALF) if i in (3, 6) else out.T if i in turned else out for i, out in enumerate(outputs)
    )


def solution(mesh):
    fine = Mesh(mesh.devices.reshape(2, 2, 4, 4, 2), AXES)
    return jax.shard_map(
        shards,
        mesh=fine,
        in_specs=(
            P(WIDE, "n"),
            P(),
            P(WIDE, None),
            P(WIDE, None),
            P("n"),
            P("n", WIDE),
            P(WIDE, "n"),
            P("n"),
            P("n", None),
            P(),
            P("n", None),
            P(None, "n"),
            P("n", WIDE),
            P("n", WIDE),
            P(WIDE, "n"),
            P(WIDE, "n"),
        ),
        out_specs=(
            P(WIDE, "n"),
            P(WIDE, "n"),
            P(WIDE, None),
            P("n"),
            P("n", WIDE),
            P(WIDE, "n"),
            P("n"),
            P("n", None),
            P(),
            P("n", None),
            P(None, "n"),
            P("n", WIDE),
            P("n", WIDE),
            P(WIDE, "n"),
        ),
        check_vma=False,
    )
```

time: 2210 us -> 349 us (0.16)
  waiting for transfers between devices: 767 us -> 0.04 us
  blocking collectives: 562 us -> 0 us
  starting transfers between devices: 339 us -> 5.77 us
  Pallas kernels: 0 us -> 315 us
  matrix products: 281 us -> 0 us
  local copies, waits for them, and re-layouts: 165 us -> 3.45 us
  other arithmetic: 57.9 us -> 4.45 us
    pallas_call x0 -> x8, Pallas kernels: none -> 315 us  [the longest x1 66.7 us: experts_step(): pl.pallas_call(kernel, out_shape=[shape_of((TOK, D), f32), shape_of((TOK,...]
    psum x1 -> x0, waiting for transfers between devices: 300 us -> none  [shards(): lax.psum(plain_dot(rows_x, up_block).astype(jnp.bfloat16), 'narrow')]
    dot_general x74 -> x0, matrix products: 281 us -> none  [the longest x58 261 us: plain_dot(): return jnp.dot(left_side, right_side, preferred_element_type=jnp.float32)]
    psum x3 -> x0, blocking collectives: 280 us -> none  [the longest x1 256 us: shards(): lax.psum((grad_gain_one, grad_gain_two, grad_w_router, grad_w_const, grad...]
    all_to_all x4 -> x0, waiting for transfers between devices: 252 us -> none  [the longest x1 76.1 us: shards(): lax.all_to_all(down_part.reshape(wide_count, -1, half_width).astype(jnp.b...]
    unnamed x2 -> x0, blocking collectives: 149 us -> none
    all_gather x7 -> x0, blocking collectives: 134 us -> none  [the longest x1 74 us: shards(): lax.all_gather(w_out, 'wide', axis=0, tiled=True)]
    ppermute x32 -> x3, starting transfers between devices: 137 us -> 5.73 us  [the longest x1 4.05 us: shards(): lax.ppermute(far_other, ('n', 'y'), [(4 * k + i, 4 * (1 - k) + j) for k i...]
  transfers between devices with their start and end apart: 74 -> 4, of which waited for: 16 -> 0; matrix products, arithmetic and copies ran while one was open for 11% -> 0% of each run, Pallas kernels for 0% -> 49%
where the time goes in v1:
time: 349 us; the launch traced here: 343 us
  Pallas kernels  315 us (90%)
  between operations  14.4 us (4%)
  starting transfers between devices  5.77 us (2%)
  other arithmetic  4.45 us (1%)
    pallas_call x1, Pallas kernels, experts_step(): pl.pallas_call(kernel, out_shape=[shape_of((TOK, D), f32), shape_of((TOK,...  66.7 us
    pallas_call x1, Pallas kernels, attend(): pl.pallas_call(kernel, out_shape=[shape_of((4, 192, TOK), bf16), shape_of...  66.4 us
    pallas_call x1, Pallas kernels, attend_backward(): pl.pallas_call(kernel, out_shape=[shape_of((4, 192, TOK), bf16), shape_of...  64.5 us
    pallas_call x1, Pallas kernels, gather_all(): pl.pallas_call(kernel, out_shape=[whole] * 3 + swap_shapes(swaps_in) + [s...  47.1 us
    pallas_call x1, Pallas kernels, scatter_sums(): pl.pallas_call(kernel, out_shape=[shape_of((3 * PART, HALF), f32), small]...  45.3 us
    pallas_call x1, Pallas kernels, middle_backward(): pl.pallas_call(kernel, out_shape=[shape_of((TOK, D), f32), shape_of((TOK,...  11.9 us
    pallas_call x1, Pallas kernels, project_forward(): pl.pallas_call(kernel, out_shape=[shape_of((3 * D, D), bf16), shape_of((D...  7.95 us
  transfers between devices with their start and end apart: 4, of which 0 were waited for; matrix products, arithmetic and copies ran while one was open for 0% of the time, Pallas kernels for 49%

profile of v1, /device:TPU:7, one launch (start us, length us, event | category | flops | bytes accessed | tf_op | source)
XLA Modules:
  0.0 342.6 jit_solution(14891820939648861586)
XLA Ops:
  7.2 0.0 copy-start.3
  7.2 0.0 copy-start.4
  7.2 0.0 all-gather.3.cloned.1.call-start
  7.2 1.1 copy.33
  8.3 1.9 pad_maximum_fusion
  10.2 0.0 all-gather.3.cloned.1.call-update
  10.3 0.0 copy-done.3
  10.3 0.6 broadcast_in_dim.6.refs_5_
  10.8 0.0 copy-done.4
  10.8 0.6 broadcast_in_dim.7.refs_6_
  11.4 47.1 %gather_weights.1 = (bf16[2,4,4,4,16,384]{5,4,3,2,1,0:T(8,128)(2,1)}, bf16[2,4,4,4,16,384]{5,4,3,2,1,0:T(8,128)(2,1)}, bf16[2,4,4,4,16,384]{5,4,3,2,1,0:T(8,128)...) custom-call(bf16[36,384]{1,0:T(8,128)(2,1)} %bitcast.28, ...), custom_call_target="tpu_custom_call" | custom-call | tf_op jit(solution)/shard_map/gather_weights/pallas_call | solution.py:286
  58.5 8.0 %project_forward.1 = (bf16[2304,768]{1,0:T(8,128)(2,1)}, bf16[768,768]{1,0:T(8,128)(2,1)}, bf16[4,192,256]{2,1,0:T(8,128)(2,1)}, bf16[4,256,384]{2,1,0:T(8,128)(...) custom-call(bf16[2,4,4,4,16,384]{5,4,3,2,1,0:T(8,128)(2,1)} %get-tuple-elem, ...), custom_call_target="tpu_custom_call" | custom-call | tf_op jit(solution)/shard_map/project_forward/pallas_call | solution.py:373
  66.4 66.4 %attend.1 = (bf16[4,192,256]{2,1,0:T(8,128)(2,1)}, bf16[4,3,128,256]{3,2,1,0:T(8,128)(2,1)}, bf16[4,2,2,256,384]{4,3,2,1,0:T(8,128)(2,1)}, f32[4,192,256]{2,1,0:...) custom-call(bf16[4,192,256]{2,1,0:T(8,128)(2,1)} %get-tuple-element.83.q_in, ...), custom_call_target="tpu_custom_call" | custom-call | tf_op jit(solution)/shard_map/attend/pallas_call | solution.py:961
  132.8 0.0 all-gather.3.cloned.1.call-done
  132.9 66.7 %experts_step.1 = (f32[256,768]{1,0:T(8,128)}, bf16[256,768]{1,0:T(8,128)(2,1)}, bf16[2,256,384]{2,1,0:T(8,128)(2,1)}, f32[256,128]{1,0:T(8,128)}, bf16[16,64,38...) custom-call(bf16[4,192,256]{2,1,0:T(8,128)(2,1)} %get-tuple-element., ...), custom_call_target="tpu_custom_call" | custom-call | tf_op jit(solution)/shard_map/experts_step/pallas_call | solution.py:625
  199.5 11.9 %middle_backward.1 = (f32[256,768]{1,0:T(8,128)}, bf16[256,768]{1,0:T(8,128)(2,1)}, bf16[4,192,256]{2,1,0:T(8,128)(2,1)}, f32[24,896]{1,0:T(8,128)}, f32[1,16,256]{2,1,0:T(8,128)}) custom-call(bf16[16,64,384]{2,1,0:T(8,128)(2,1)} %get-tuple-element.92.rows_ref, bf16[1024,512]{1,0:T(8,128)(2,1)} %get-tuple-element.90.hit_ref, ...), custom_call_target="tpu_custom_call" | custom-call | tf_op jit(solution)/shard_map/middle_backward/pallas_call | solution.py:766
  211.4 0.0 copy-start.6
  211.5 0.0 copy-start.5
  211.5 64.5 %attend_backward.1 = (bf16[4,192,256]{2,1,0:T(8,128)(2,1)}, bf16[4,256,384]{2,1,0:T(8,128)(2,1)}, bf16[16,64,384]{2,1,0:T(8,128)(2,1)}, f32[24,896]{1,0:T(8,128)...) custom-call(bf16[4,192,256]{2,1,0:T(8,128)(2,1)} %get-tuple-element., ...), custom_call_target="tpu_custom_call" | custom-call | tf_op jit(solution)/shard_map/attend_backward/pallas_call | solution.py:1181
  276.0 1.7 collective-permute-start
  277.6 0.0 copy-done.6
  277.6 0.0 collective-permute-start.1
  277.6 0.0 copy-done.5
  277.7 4.1 %collective-permute-start.2 = (bf16[3,384,256]{2,1,0:T(8,128)(2,1)S(1)}, bf16[3,384,256]{2,1,0:T(8,128)(2,1)S(1)}, u32[]{:S(2)}, u32[]{:S(2)}) collective-permute-start(bf16[3,384,256]{2,1,0:T(8,128)(2,1)S(1)} %copy-done.5), channel_id=1, source_target_pairs={{0,68},{2,70},{4,64},{6,66},{64,4},{66,6},{68,0},{70,2},{1,69},{3,... | collective-permute-start | bytes 1769480 | tf_op jit(solution)/shard_map/ppermute | solution.py:1558
  281.7 45.3 %scatter_sums.1 = (f32[48,384]{1,0:T(8,128)}, f32[8,768]{1,0:T(8,128)}, bf16[2,256,384]{2,1,0:T(8,128)(2,1)}) custom-call(bf16[4,192,256]{2,1,0:T(8,128)(2,1)} %get-tuple-element.108.refs_0_, bf16[4,256,384]{2,1,0:T(8,128)(2,1)} %get-tuple-element.109.refs_1_, f32[4,192,256]{2,1,0:T(8,128)} %get-tuple-element.110.refs_2_, ...), custom_call_target="tpu_custom_call" | custom-call | tf_op jit(solution)/shard_map/scatter_sums/pallas_call | solution.py:1435
  327.0 0.0 collective-permute-done.s1_ref
  327.0 0.0 copy-start
  327.0 0.0 collective-permute-done.1.s2_ref
  327.1 0.0 copy-start.1
  327.1 0.0 collective-permute-done.2.s3_ref
  327.1 0.0 copy-start.2
  327.1 0.8 copy-done
  327.8 0.2 copy-done.1
  328.1 0.2 copy-done.2
  328.3 4.7 %finish.1 = (bf16[512,384]{1,0:T(8,128)(2,1)}, f32[512,384]{1,0:T(8,128)}, f32[12,512]{1,0:T(8,128)}, f32[1,384]{1,0:T(1,128)}, f32[36,384]{1,0:T(8,128)}, /*ind...) custom-call(f32[48,384]{1,0:T(8,128)} %get-tuple-element.117.block_r, ...), custom_call_target="tpu_custom_call" | custom-call | tf_op jit(solution)/shard_map/finish/pallas_call | solution.py:1509
  333.0 1.3 reduce
  334.3 1.3 reduce.1
Async XLA Ops:
  7.2 3.1 copy-start.3
  7.2 3.6 %copy-start.4 = (bf16[384]{0:T(512)(128)(2,1)S(1)}, bf16[384]{0:T(512)(128)(2,1)}, u32[]{:S(2)}) copy-start(bf16[384]{0:T(512)(128)(2,1)} %param.23) | copy-start | bytes 2308
  7.2 125.7 %all-gather.3.cloned.1.call-start = ((), (), s32[]{:S(2)}) async-start(), calls=%async_computation | async-start | bytes 10027008 | tf_op jit(solution)/shard_map/all_gather | solution.py:1538
  211.4 66.2 %copy-start.6 = (bf16[3,384,256]{2,1,0:T(8,128)(2,1)S(1)}, bf16[3,384,256]{2,1,0:T(8,128)(2,1)}, u32[]{:S(2)}) copy-start(bf16[3,384,256]{2,1,0:T(8,128)(2,1)} %get-tuple-element.124) | copy-start | bytes 1769476
  211.5 66.2 %copy-start.5 = (bf16[3,384,256]{2,1,0:T(8,128)(2,1)S(1)}, bf16[3,384,256]{2,1,0:T(8,128)(2,1)}, u32[]{:S(2)}) copy-start(bf16[3,384,256]{2,1,0:T(8,128)(2,1)} %get-tuple-element.125) | copy-start | bytes 1769476
  276.0 51.1 %collective-permute-start = (bf16[3,384,256]{2,1,0:T(8,128)(2,1)}, bf16[3,384,256]{2,1,0:T(8,128)(2,1)S(1)}, u32[]{:S(2)}, u32[]{:S(2)}) collective-permute-start(bf16[3,384,256]{2,1,0:T(8,128)(2,1)} %get-tuple-element.123), channel_id=1, source_target_pairs={{0,64},{64,0},{1,65},{65,1},{2,66},{66,2},{3,67},{67,3},{4,68},{68... | collective-permute-start | bytes 1769480 | tf_op jit(solution)/shard_map/ppermute | solution.py:1568
  277.6 49.4 %collective-permute-start.1 = (bf16[3,384,256]{2,1,0:T(8,128)(2,1)S(1)}, bf16[3,384,256]{2,1,0:T(8,128)(2,1)S(1)}, u32[]{:S(2)}, u32[]{:S(2)}) collective-permute-start(bf16[3,384,256]{2,1,0:T(8,128)(2,1)S(1)} %copy-done.6), channel_id=1, source_target_pairs={{0,4},{2,6},{4,0},{6,2},{1,5},{3,7},{5,1},{7,3},{8,12},{10,14},{12... | collective-permute-start | bytes 1769480 | tf_op jit(solution)/shard_map/ppermute | solution.py:1557
  277.7 49.4 %collective-permute-start.2 = (bf16[3,384,256]{2,1,0:T(8,128)(2,1)S(1)}, bf16[3,384,256]{2,1,0:T(8,128)(2,1)S(1)}, u32[]{:S(2)}, u32[]{:S(2)}) collective-permute-start(bf16[3,384,256]{2,1,0:T(8,128)(2,1)S(1)} %copy-done.5), channel_id=1, source_target_pairs={{0,68},{2,70},{4,64},{6,66},{64,4},{66,6},{68,0},{70,2},{1,69},{3,... | collective-permute-start | bytes 1769480 | tf_op jit(solution)/shard_map/ppermute | solution.py:1558
  327.0 0.8 copy-start
  327.1 1.0 copy-start.1
  327.1 1.2 copy-start.2
Sparse Core Ops, SparseCore 0:
  10.5 113.3 all-gather.2
